TPU v7x, 32 devices: a whole 2x2x4 slice. The times are simulated.
32 devices in a mesh: prow: 4 (over y, core), pcol: 8 (over z, x).
Axes of the slice: x: 2, y: 2, z: 4, core: 2. Of those that a mesh axis runs over, the one named last changes fastest.
Arguments:
- coords: float32 [2, 8, 2048], P(None, None, 'prow'), may hold values from 0 to 1
- observations: float32 [8, 2048], P(None, 'prow'), may hold values from -6 to 6
- length_scale: float32 [1], replicated, may hold values from 0.06 to 0.15
- nugget: float32 [1], replicated, may hold values from 0.3 to 1
Outputs:
- slab: float32 [8, 2048, 1024], P(None, 'prow', 'pcol')
- whitened: float32 [8, 2048], P(None, 'prow')
- loglik_part: float32 [1], replicated
All inputs are finite; a program needn't handle non-finite values.
Results may differ from a plain program's by a relative error of at most 0.0003.
Values sent between devices are 32-bit elements; how exact they have to be, the bound alone decides.
No kernel may reach another device: no remote copies, remote signals or barrier semaphores. Data moves between devices by JAX's collectives and lax.ppermute only.
A program may use at most 128 MiB of HBM per device.

v0:
```python
import math

import jax
import jax.numpy as jnp
from jax import lax
from jax.sharding import PartitionSpec as P

SLAB_DEV = 128


SQRT_THREE = math.sqrt(3.0)


def matern_block(left_xy, right_xy, decay_rate):
    delta_x = left_xy[0][:, None] - right_xy[0][None, :]
    delta_y = left_xy[1][:, None] - right_xy[1][None, :]
    scaled = decay_rate * jnp.sqrt(delta_x * delta_x + delta_y * delta_y)
    return (1.0 + scaled) * jnp.exp(-scaled)


def covariance(left_xy, left_ids, right_xy, right_ids, decay_rate, nugget_value):
    same = (left_ids[:, None] == right_ids[None, :]).astype(jnp.float32)
    return matern_block(left_xy, right_xy, decay_rate) + nugget_value * same


def transposed_product(left, right):
    return jnp.dot(
        left, right.T, precision=lax.Precision.HIGHEST, preferred_element_type=jnp.float32
    )


def vector_product(matrix, vector):
    return jnp.dot(
        matrix, vector, precision=lax.Precision.HIGHEST, preferred_element_type=jnp.float32
    )


def inverse_lower(factor):
    identity = jnp.eye(factor.shape[0], dtype=jnp.float32)
    return jax.scipy.linalg.solve_triangular(factor, identity, lower=True)


def shards(coords, observations, length_scale, nugget):
    row_procs = lax.axis_size("prow")
    col_procs = lax.axis_size("pcol")
    row_rank = lax.axis_index("prow")
    col_rank = lax.axis_index("pcol")
    tile_count = coords.shape[1]
    block_size = coords.shape[2]
    slab_width = SLAB_DEV
    decay_rate = SQRT_THREE / length_scale[0]
    nugget_value = nugget[0]
    leading_xy, leading_obs = (
        lax.all_gather(coords[:, 0, :], "prow", axis=1, tiled=True),
        lax.all_gather(observations[0, :], "prow", axis=0, tiled=True),
    )
    leading_ids = jnp.arange(row_procs * block_size, dtype=jnp.int32)
    first_xy = leading_xy[:, :block_size]
    first_ids = leading_ids[:block_size]
    second_xy = leading_xy[:, block_size : 2 * block_size]
    second_ids = leading_ids[block_size : 2 * block_size]
    factor_first = jnp.linalg.cholesky(
        covariance(first_xy, first_ids, first_xy, first_ids, decay_rate, nugget_value)
    )
    inverse_first = inverse_lower(factor_first)
    second_on_first = transposed_product(
        covariance(second_xy, second_ids, first_xy, first_ids, decay_rate, nugget_value),
        inverse_first,
    )
    schur_second = covariance(
        second_xy, second_ids, second_xy, second_ids, decay_rate, nugget_value
    ) - transposed_product(second_on_first, second_on_first)
    factor_second = jnp.linalg.cholesky(schur_second)
    inverse_second = inverse_lower(factor_second)
    whitened_first = vector_product(inverse_first, leading_obs[:block_size])
    whitened_second = vector_product(
        inverse_second,
        leading_obs[block_size : 2 * block_size] - vector_product(second_on_first, whitened_first),
    )
    quadratic = 0.5 * (
        jnp.sum(whitened_first * whitened_first) + jnp.sum(whitened_second * whitened_second)
    )
    log_terms = jnp.sum(jnp.log(jnp.diagonal(factor_first))) + jnp.sum(
        jnp.log(jnp.diagonal(factor_second))
    )
    loglik_part = -(quadratic + log_terms) / (2.0 * block_size)

    def compute_first(rows_xy, rows_ids):
        raw_rows = transposed_product(
            covariance(rows_xy, rows_ids, first_xy, first_ids, decay_rate, nugget_value),
            inverse_first,
        )
        inside = jnp.take(factor_first, rows_ids % block_size, axis=0)
        return jnp.where((rows_ids < block_size)[:, None], inside, raw_rows)

    def compute_second(rows_xy, rows_ids, rows_first):
        schur_rows = covariance(
            rows_xy, rows_ids, second_xy, second_ids, decay_rate, nugget_value
        ) - transposed_product(rows_first, second_on_first)
        raw_rows = transposed_product(schur_rows, inverse_second)
        inside = jnp.take(factor_second, rows_ids % block_size, axis=0)
        result = jnp.where((rows_ids < 2 * block_size)[:, None], inside, raw_rows)
        return jnp.where((rows_ids < block_size)[:, None], 0.0, result)

    local_xy = coords.reshape(2, tile_count * block_size)
    local_obs = observations.reshape(tile_count * block_size)
    tile_number = jnp.arange(tile_count, dtype=jnp.int32)[:, None]
    offsets = jnp.arange(block_size, dtype=jnp.int32)[None, :]
    local_ids = ((tile_number * row_procs + row_rank) * block_size + offsets).reshape(
        tile_count * block_size
    )
    share_rows = tile_count * block_size // col_procs
    share_first_row = col_rank * share_rows
    share_xy = lax.dynamic_slice_in_dim(local_xy, share_first_row, share_rows, 1)
    share_ids = lax.dynamic_slice_in_dim(local_ids, share_first_row, share_rows, 0)
    share_obs = lax.dynamic_slice_in_dim(local_obs, share_first_row, share_rows, 0)
    column_first_site = 2 * block_size + col_rank * slab_width
    column_xy = lax.dynamic_slice_in_dim(leading_xy, column_first_site, slab_width, 1)
    column_ids = column_first_site + jnp.arange(slab_width, dtype=jnp.int32)
    column_first = compute_first(column_xy, column_ids)
    column_second = compute_second(column_xy, column_ids, column_first)
    share_first = compute_first(share_xy, share_ids)
    local_first = lax.all_gather(share_first, "pcol", axis=0, tiled=True)
    share_second = compute_second(share_xy, share_ids, share_first)
    remainder = (
        share_obs
        - vector_product(share_first, whitened_first)
        - vector_product(share_second, whitened_second)
    )
    inside_first = jnp.take(whitened_first, share_ids % block_size)
    inside_second = jnp.take(whitened_second, share_ids % block_size)
    share_white = jnp.where(
        share_ids < block_size,
        inside_first,
        jnp.where(share_ids < 2 * block_size, inside_second, remainder),
    )
    local_second, local_white = (
        lax.all_gather(share_second, "pcol", axis=0, tiled=True),
        lax.all_gather(share_white, "pcol", axis=0, tiled=True),
    )
    value = covariance(local_xy, local_ids, column_xy, column_ids, decay_rate, nugget_value)
    value = (
        value
        - transposed_product(local_first, column_first)
        - transposed_product(local_second, column_second)
    )
    local_slab = jnp.where((local_ids < 2 * block_size)[:, None], 0.0, value)
    return (
        local_slab.reshape(tile_count, block_size, slab_width),
        local_white.reshape(tile_count, block_size),
        loglik_part.reshape(1),
    )


def solution(mesh):
    placed = (P(None, None, "prow"), P(None, "prow"), P(), P())
    return jax.shard_map(
        shards,
        mesh=mesh,
        in_specs=placed,
        out_specs=(P(None, "prow", "pcol"), P(None, "prow"), P()),
        check_vma=False,
    )
```

profile of v0, /device:TPU:0, one launch (start us, length us, event | category | flops | bytes accessed | tf_op | source)
XLA Modules:
  0.0 497.5 jit_solution(14735290283101741804)
XLA Ops:
  9.9 6.1 %all-gather = f32[2,1,2048]{2,1,0:T(1,128)S(1)} all-gather(f32[2,1,512]{2,1,0:T(1,128)S(1)} %slice.171), channel_id=2, replica_groups=mesh['prow'=4,'pcol'=8] {'prow'}, dimensions={2}, use_global_device_ids=true | all-gather | bytes 20480 | tf_op jit(solution)/shard_map/all_gather | solution.py:54
  19.7 11.7 %cholesky.286 = f32[128,128]{1,0:T(8,128)S(1)} custom-call(f32[128,128]{1,0:T(8,128)S(1)} %cholesky.426), custom_call_target="Cholesky" | custom-call | tf_op jit(solution)/shard_map/jit(cholesky)/cholesky | solution.py:62
  31.4 9.8 %custom-call.31 = f32[1,128,128]{1,2,0:T(8,128)S(1)} custom-call(f32[1,128,128]{2,1,0:T(8,128)S(1)} %get-tuple-element.71), custom_call_target="InvertDiagBlocksLowerTriangular" | custom-call | tf_op jit(solution)/shard_map/jit(cholesky)/cholesky | solution.py:62
  42.0 11.9 %cholesky.305 = f32[128,128]{1,0:T(8,128)S(1)} custom-call(f32[128,128]{1,0:T(8,128)S(1)} %cholesky.430), custom_call_target="Cholesky" | custom-call | tf_op jit(solution)/shard_map/jit(cholesky)/cholesky | solution.py:62
  54.0 9.8 %custom-call.32 = f32[1,128,128]{1,2,0:T(8,128)S(1)} custom-call(f32[1,128,128]{2,1,0:T(8,128)S(1)} %get-tuple-element.68), custom_call_target="InvertDiagBlocksLowerTriangular" | custom-call | tf_op jit(solution)/shard_map/jit(cholesky)/cholesky | solution.py:62
  64.5 11.7 %cholesky.326 = f32[128,128]{1,0:T(8,128)S(1)} custom-call(f32[128,128]{1,0:T(8,128)S(1)} %cholesky.435), custom_call_target="Cholesky" | custom-call | tf_op jit(solution)/shard_map/jit(cholesky)/cholesky | solution.py:62
  76.9 9.8 %custom-call.33 = f32[1,128,128]{1,2,0:T(8,128)S(1)} custom-call(f32[1,128,128]{2,1,0:T(8,128)S(1)} %get-tuple-element.65), custom_call_target="InvertDiagBlocksLowerTriangular" | custom-call | tf_op jit(solution)/shard_map/jit(cholesky)/cholesky | solution.py:62
  87.3 12.1 %cholesky.343 = f32[128,128]{1,0:T(8,128)S(1)} custom-call(f32[128,128]{1,0:T(8,128)S(1)} %convolution_subtract_fusion.16), custom_call_target="Cholesky" | custom-call | tf_op jit(solution)/shard_map/jit(cholesky)/cholesky | solution.py:62
  104.5 11.6 %while.4 = (s32[]{:T(128)}, f32[512,512]{1,0:T(8,128)}, s32[4,2]{0,1:T(2,128)S(1)}, f32[4,128,128]{2,1,0:T(8,128)S(1)}, s32[]{:T(128)}) while((s32[]{:T(128)}, f32[512,512]{1,0:T(8,128)}, s32[4,2]{0,1:T(2,128)S(1)}, f32[4,128,128]{2,1,0:T(8,128)S(1)}, s32[]{:T(128)}) %tuple.70), condition=%wide.while_cond, body=%wide.while_body.sunk | while | flops 2 | bytes 131189 | solution.py:40
  116.1 39.3 %custom-call.34 = f32[4,128,128]{1,2,0:T(8,128)S(1)} custom-call(f32[4,128,128]{2,1,0:T(8,128)S(1)} %get-tuple-element.22), custom_call_target="InvertDiagBlocksLowerTriangular" | custom-call | tf_op jit(solution)/shard_map/jit(_solve_triangular)/triangular_solve | solution.py:40
  166.0 5.1 %convolution_select_fusion.1 = f32[512,512]{0,1:T(8,128)} fusion(f32[512,512]{0,1:T(8,128)} %copy.22, s32[512]{0:T(512)S(1)} %get-tuple-element.43, f32[512]{0:T(512)S(1)} %bitcast.220, f32[512]{0:T(512)S(1)} %bitcast.218, f32[]{:T(128)} %bitcast.173, f32[512]{0:T(512)S(1)} %bitcast.191, f32[512]{0:T(512)S(1)} %bitcast.196, f32[]{:T(128)} %bitcast, ...), kind=kOutput, calls=%fused_computation.19 | convolution fusion | flops 1615069184 | bytes 3159048 | tf_op jit(solution)/shard_map/dot_general | solution.py:27
  171.5 4.1 fusion.7
  183.0 11.7 %cholesky.358 = f32[128,128]{1,0:T(8,128)S(1)} custom-call(f32[128,128]{1,0:T(8,128)S(1)} %cholesky.439), custom_call_target="Cholesky" | custom-call | tf_op jit(solution)/shard_map/jit(cholesky)/cholesky | solution.py:73
  195.3 10.2 %custom-call.35 = f32[1,128,128]{1,2,0:T(8,128)S(1)} custom-call(f32[1,128,128]{2,1,0:T(8,128)S(1)} %get-tuple-element.61), custom_call_target="InvertDiagBlocksLowerTriangular" | custom-call | tf_op jit(solution)/shard_map/jit(cholesky)/cholesky | solution.py:73
  208.1 11.7 %cholesky.377 = f32[128,128]{1,0:T(8,128)S(1)} custom-call(f32[128,128]{1,0:T(8,128)S(1)} %cholesky.443), custom_call_target="Cholesky" | custom-call | tf_op jit(solution)/shard_map/jit(cholesky)/cholesky | solution.py:73
  220.4 9.8 %custom-call.36 = f32[1,128,128]{1,2,0:T(8,128)S(1)} custom-call(f32[1,128,128]{2,1,0:T(8,128)S(1)} %get-tuple-element.58), custom_call_target="InvertDiagBlocksLowerTriangular" | custom-call | tf_op jit(solution)/shard_map/jit(cholesky)/cholesky | solution.py:73
  231.7 11.7 %cholesky.398 = f32[128,128]{1,0:T(8,128)S(1)} custom-call(f32[128,128]{1,0:T(8,128)S(1)} %cholesky.448), custom_call_target="Cholesky" | custom-call | tf_op jit(solution)/shard_map/jit(cholesky)/cholesky | solution.py:73
  243.5 10.0 %custom-call.37 = f32[1,128,128]{1,2,0:T(8,128)S(1)} custom-call(f32[1,128,128]{2,1,0:T(8,128)S(1)} %get-tuple-element.55), custom_call_target="InvertDiagBlocksLowerTriangular" | custom-call | tf_op jit(solution)/shard_map/jit(cholesky)/cholesky | solution.py:73
  254.9 11.7 %cholesky.415 = f32[128,128]{1,0:T(8,128)S(1)} custom-call(f32[128,128]{1,0:T(8,128)S(1)} %convolution_subtract_fusion.15), custom_call_target="Cholesky" | custom-call | tf_op jit(solution)/shard_map/jit(cholesky)/cholesky | solution.py:73
  273.2 2.6 fusion.5
  275.9 11.2 %while.5 = (s32[]{:T(128)}, f32[512,512]{1,0:T(8,128)}, s32[4,2]{0,1:T(2,128)S(1)}, f32[4,128,128]{2,1,0:T(8,128)S(1)}, s32[]{:T(128)}) while((s32[]{:T(128)}, f32[512,512]{1,0:T(8,128)}, s32[4,2]{0,1:T(2,128)S(1)}, f32[4,128,128]{2,1,0:T(8,128)S(1)}, s32[]{:T(128)}) %tuple.80), condition=%wide.while_cond.clone, body=%wide.while_body.clone.sunk | while | flops 2 | bytes 131189 | solution.py:40
  287.1 39.9 %custom-call.38 = f32[4,128,128]{1,2,0:T(8,128)} custom-call(f32[4,128,128]{2,1,0:T(8,128)S(1)} %get-tuple-element.23), custom_call_target="InvertDiagBlocksLowerTriangular" | custom-call | tf_op jit(solution)/shard_map/jit(_solve_triangular)/triangular_solve | solution.py:40
  342.4 2.9 fusion.1
  345.3 4.5 gather_fusion
  349.8 4.5 gather_fusion.1
  357.3 5.7 %all-gather.1 = f32[1,2048]{1,0:T(1,128)S(1)} all-gather(f32[1,512]{1,0:T(1,128)S(1)} %slice-done), channel_id=3, replica_groups=mesh['prow'=4,'pcol'=8] {'prow'}, dimensions={1}, use_global_device_ids=true | all-gather | bytes 10240 | tf_op jit(solution)/shard_map/all_gather | solution.py:55
  365.3 3.5 gather_fusion.6
  371.9 3.5 gather_fusion.7
  381.9 26.9 %all-gather.2 = f32[8,1,512]{2,1,0:T(1,128)S(1)} all-gather(f32[1,1,512]{2,1,0:T(1,128)S(1)} %bitcast.215), channel_id=1, replica_groups=mesh['prow'=4,'pcol'=8] {'pcol'}, dimensions={0}, use_global_device_ids=true | all-gather | bytes 18432 | tf_op jit(solution)/shard_map/all_gather | solution.py:139
  414.6 16.9 %convolution_subtract_fusion.1 = f32[4096,128]{1,0:T(8,128)S(1)} fusion(f32[4096,512]{0,1:T(8,128)} %all-gather.6.cloned.1.call-done, f32[128,512]{1,0:T(8,128)} %copy-done.18, f32[]{:T(128)} %bitcast.167, s32[128]{0:T(128)S(1)} %iota_add_fusion.2, f32[128]{0:T(128)S(1)} %get-tuple-element.81, f32[4096]{0:T(1024)S(1)} %bitcast.187, ...), kind=kOutput, calls=%fused_computation.14 | convolution fusion | flops 3228041216 | bytes 10798600 | tf_op jit(solution)/shard_map/dot_general | solution.py:27
  431.5 40.7 %all-gather.8.cloned.1.call-done = f32[4096,512]{0,1:T(8,128)} async-done(((f32[512,512]{0,1:T(8,128)}), f32[4096,512]{0,1:T(8,128)}) %all-gather.8.cloned.1.call-update) | async-done | bytes 8388624 | tf_op jit(solution)/shard_map/all_gather | solution.py:138
  472.2 16.9 %fusion = f32[4096,128]{1,0:T(8,128)} fusion(f32[4096,128]{1,0:T(8,128)S(1)} %convolution_subtract_fusion.1, f32[4096,512]{0,1:T(8,128)} %all-gather.8.cloned.1.call-done, f32[128,512]{1,0:T(8,128)S(1)} %fusion.2, pred[4096]{0:T(1024)(128)(4,1)S(1)} %broadcast_compare_fusion), kind=kOutput, calls=%fused_computation.13 | convolution fusion | flops 3222274048 | bytes 12849152 | tf_op jit(solution)/shard_map/dot_general | solution.py:27
  (226 shorter events, 94.7 us)
Async XLA Ops:
  7.2 407.4 %all-gather.6.cloned.1.call-start = ((), (), s32[]{:S(2)}) async-start(), calls=%async_computation | async-start | bytes 9437184 | tf_op jit(solution)/shard_map/all_gather | solution.py:123
  16.1 323.8 %copy-start.30 = (f32[1,512]{1,0:T(1,128)}, f32[1,512]{1,0:T(1,128)S(1)}, u32[]{:S(2)}) copy-start(f32[1,512]{1,0:T(1,128)S(1)} %get-tuple-element.76) | copy-start | bytes 6148
  16.1 323.8 %copy-start.32 = (f32[1,512]{1,0:T(1,128)}, f32[1,512]{1,0:T(1,128)S(1)}, u32[]{:S(2)}) copy-start(f32[1,512]{1,0:T(1,128)S(1)} %get-tuple-element.79) | copy-start | bytes 6148
  16.3 326.1 %copy-start.34 = (pred[512]{0:T(512)(128)(4,1)}, pred[512]{0:T(512)(128)(4,1)S(1)}, u32[]{:S(2)}) copy-start(pred[512]{0:T(512)(128)(4,1)S(1)} %get-tuple-element.42) | copy-start | bytes 1540
  16.3 149.7 %copy-start.38 = (pred[512]{0:T(512)(128)(4,1)}, pred[512]{0:T(512)(128)(4,1)S(1)}, u32[]{:S(2)}) copy-start(pred[512]{0:T(512)(128)(4,1)S(1)} %get-tuple-element.82) | copy-start | bytes 1540
  16.3 326.0 %copy-start.36 = (pred[512]{0:T(512)(128)(4,1)}, pred[512]{0:T(512)(128)(4,1)S(1)}, u32[]{:S(2)}) copy-start(pred[512]{0:T(512)(128)(4,1)S(1)} %get-tuple-element.46) | copy-start | bytes 1540
  64.4 40.0 %copy-start.42 = (s32[4]{0:T(128)S(1)}, s32[4]{0:T(128)}, u32[]{:S(2)}) copy-start(s32[4]{0:T(128)} %iota_multiply_fusion) | copy-start | bytes 52
  155.8 15.6 %copy-start.11 = (f32[128,512]{1,0:T(8,128)}, f32[128,512]{1,0:T(8,128)S(1)}, u32[]{:S(2)}) copy-start(f32[128,512]{1,0:T(8,128)S(1)} %fusion.91) | copy-start | bytes 786436
  166.0 5.5 %copy-start.17 = (f32[128,512]{1,0:T(8,128)S(1)}, f32[128,512]{1,0:T(8,128)}, u32[]{:S(2)}) copy-start(f32[128,512]{1,0:T(8,128)} %copy-done.16) | copy-start | bytes 786436
  166.0 5.5 %copy-start.22 = (f32[128,512]{1,0:T(8,128)S(1)}, f32[128,512]{1,0:T(8,128)}, u32[]{:S(2)}) copy-start(f32[128,512]{1,0:T(8,128)} %copy-done.21) | copy-start | bytes 786436
  166.0 5.5 %copy-start.25 = (f32[128,512]{1,0:T(8,128)S(1)}, f32[128,512]{1,0:T(8,128)}, u32[]{:S(2)}) copy-start(f32[128,512]{1,0:T(8,128)} %fusion.124) | copy-start | bytes 786436
  171.2 301.0 %all-gather.8.cloned.1.call-start = ((), (), s32[]{:S(2)}) async-start(), calls=%async_computation.1 | async-start | bytes 9437184 | tf_op jit(solution)/shard_map/all_gather | solution.py:138
  171.4 168.5 %copy-start.28 = (s32[512]{0:T(512)}, s32[512]{0:T(512)S(1)}, u32[]{:S(2)}) copy-start(s32[512]{0:T(512)S(1)} %iota_add_fusion) | copy-start | bytes 6148
  331.9 5.4 %copy-start.24 = (f32[4,128,128]{1,2,0:T(8,128)S(1)}, f32[4,128,128]{1,2,0:T(8,128)}, u32[]{:S(2)}) copy-start(f32[4,128,128]{1,2,0:T(8,128)} %custom-call.38) | copy-start | bytes 786436
  334.4 5.5 %copy-start.3 = (f32[512,512]{0,1:T(8,128)S(1)}, f32[512,512]{0,1:T(8,128)}, u32[]{:S(2)}) copy-start(f32[512,512]{0,1:T(8,128)} %convolution_select_fusion.1) | copy-start | bytes 3145732
  334.5 5.5 %copy-start.6 = (f32[512,512]{1,0:T(8,128)S(1)}, f32[512,512]{1,0:T(8,128)}, u32[]{:S(2)}) copy-start(f32[512,512]{1,0:T(8,128)} %copy-done.5) | copy-start | bytes 3145732
  334.5 5.5 %copy-start.41 = (f32[1,512]{1,0:T(1,128)S(1)}, f32[1,512]{1,0:T(1,128)}, u32[]{:S(2)}) copy-start(f32[1,512]{1,0:T(1,128)} %copy-done.40) | copy-start | bytes 6148
  335.9 6.5 %copy-start.9 = (f32[128,512]{1,0:T(8,128)}, f32[128,512]{1,0:T(8,128)S(1)}, u32[]{:S(2)}) copy-start(f32[128,512]{1,0:T(8,128)S(1)} %fusion.121) | copy-start | bytes 786436
  354.4 8.6 %copy-start.27 = (f32[8,512]{1,0:T(8,128)S(1)}, f32[8,512]{1,0:T(8,128)}, u32[]{:S(2)}) copy-start(f32[8,512]{1,0:T(8,128)} %param.14) | copy-start | bytes 49156
  354.4 8.6 %copy-start.26 = (f32[2,8,512]{2,1,0:T(8,128)S(1)}, f32[2,8,512]{2,1,0:T(8,128)}, u32[]{:S(2)}) copy-start(f32[2,8,512]{2,1,0:T(8,128)} %param.13) | copy-start | bytes 98308
  355.9 7.2 %copy-start.12 = (f32[128,512]{1,0:T(8,128)S(1)}, f32[128,512]{1,0:T(8,128)}, u32[]{:S(2)}) copy-start(f32[128,512]{1,0:T(8,128)} %copy-done.11) | copy-start | bytes 786436
  357.3 11.5 %copy-start.7 = (f32[512,512]{1,0:T(8,128)S(1)}, f32[512,512]{1,0:T(8,128)}, u32[]{:S(2)}) copy-start(f32[512,512]{1,0:T(8,128)} %copy-done.5) | copy-start | bytes 3145732
  363.1 6.7 %copy-start.10 = (f32[128,512]{1,0:T(8,128)S(1)}, f32[128,512]{1,0:T(8,128)}, u32[]{:S(2)}) copy-start(f32[128,512]{1,0:T(8,128)} %copy-done.9) | copy-start | bytes 786436
  363.1 6.7 %copy-start.15 = (f32[128,512]{1,0:T(8,128)S(1)}, f32[128,512]{1,0:T(8,128)}, u32[]{:S(2)}) copy-start(f32[128,512]{1,0:T(8,128)} %copy-done.14) | copy-start | bytes 786436
  369.8 10.7 %copy-start.4 = (f32[512,512]{0,1:T(8,128)S(1)}, f32[512,512]{0,1:T(8,128)}, u32[]{:S(2)}) copy-start(f32[512,512]{0,1:T(8,128)} %convolution_select_fusion.1) | copy-start | bytes 3145732
  369.8 11.3 %copy-start = (f32[512,512]{0,1:T(8,128)S(1)}, f32[512,512]{0,1:T(8,128)}, u32[]{:S(2)}) copy-start(f32[512,512]{0,1:T(8,128)} %fusion.1) | copy-start | bytes 3145732
  371.9 9.9 %copy-start.35 = (pred[512]{0:T(512)(128)(4,1)S(1)}, pred[512]{0:T(512)(128)(4,1)}, u32[]{:S(2)}) copy-start(pred[512]{0:T(512)(128)(4,1)} %copy-done.34) | copy-start | bytes 1540
  371.9 9.9 %copy-start.37 = (pred[512]{0:T(512)(128)(4,1)S(1)}, pred[512]{0:T(512)(128)(4,1)}, u32[]{:S(2)}) copy-start(pred[512]{0:T(512)(128)(4,1)} %copy-done.36) | copy-start | bytes 1540
  381.1 31.0 %copy-start.8 = (f32[512,512]{1,0:T(8,128)S(1)}, f32[512,512]{1,0:T(8,128)}, u32[]{:S(2)}) copy-start(f32[512,512]{1,0:T(8,128)} %copy-done.5) | copy-start | bytes 3145732
  381.1 31.0 %copy-start.29 = (s32[512]{0:T(512)S(1)}, s32[512]{0:T(512)}, u32[]{:S(2)}) copy-start(s32[512]{0:T(512)} %copy-done.28) | copy-start | bytes 6148
  381.1 31.0 %copy-start.31 = (f32[1,512]{1,0:T(1,128)S(1)}, f32[1,512]{1,0:T(1,128)}, u32[]{:S(2)}) copy-start(f32[1,512]{1,0:T(1,128)} %copy-done.30) | copy-start | bytes 6148
  381.1 31.0 %copy-start.33 = (f32[1,512]{1,0:T(1,128)S(1)}, f32[1,512]{1,0:T(1,128)}, u32[]{:S(2)}) copy-start(f32[1,512]{1,0:T(1,128)} %copy-done.32) | copy-start | bytes 6148
  (14 other events, 41.4 us)
Sparse Core Ops, SparseCore 0:
  171.3 127.1 all-gather.5
  345.4 126.7 all-gather.7
where the time goes:
time: 508 us; the launch traced here: 497 us
  other arithmetic  250 us (49%)
  matrix products  84.1 us (17%)
  local copies, waits for them, and re-layouts  57.2 us (11%)
  waiting for transfers between devices  40.8 us (8%)
  blocking collectives  38.7 us (8%)
  between operations  25.9 us (5%)
    another operation x5, other arithmetic, inverse_lower(): return jax.scipy.linalg.solve_triangular(factor, identity, lower=True)  83.6 us
    another operation x15, other arithmetic, shards(): factor_second = jnp.linalg.cholesky(schur_second)  81.9 us
    another operation x14, other arithmetic, shards(): jnp.linalg.cholesky(covariance(first_xy, first_ids, first_xy, first_ids,...  78.9 us
    dot_general x10, matrix products, transposed_product(): jnp.dot(left, right.T, precision=lax.Precision.HIGHEST, preferred_element...  55.6 us
    all_gather x1, waiting for transfers between devices, shards(): lax.all_gather(share_second, 'pcol', axis=0, tiled=True)  40.7 us
    all_gather x1, blocking collectives, shards(): lax.all_gather(share_white, 'pcol', axis=0, tiled=True)  26.9 us
    another operation x27, local copies, waits for them, and re-layouts, inverse_lower(): return jax.scipy.linalg.solve_triangular(factor, identity, lower=True)  22.7 us
    another operation x14, matrix products, inverse_lower(): return jax.scipy.linalg.solve_triangular(factor, identity, lower=True)  14.6 us
  transfers between devices with their start and end apart: 2, of which 1 were waited for; matrix products, arithmetic and copies ran while one was open for 44% of the time, Pallas kernels for 0%

commit v1 on v0

v1 whole, which is shorter than its diff:
```python
import functools

import jax
import jax.numpy as jnp
from jax import lax
from jax.experimental import pallas as pl
from jax.experimental.pallas import tpu as pltpu
from jax.sharding import PartitionSpec as P

SLAB_DEV = 128
NB = 128
SUB = 8


def lane_bcast(v, c):
    return jnp.broadcast_to(v[:, c : c + 1], v.shape)


def row_bcast(v, k):
    return jnp.broadcast_to(v[k : k + 1, :], v.shape)


def split2(x):
    hi = x.astype(jnp.bfloat16)
    lo = (x - hi.astype(jnp.float32)).astype(jnp.bfloat16)
    return hi, lo


def dot_f32(a, b):
    return jnp.dot(a, b, preferred_element_type=jnp.float32)


def dot3(a, b):
    ah, al = split2(a)
    bh, bl = split2(b)
    return dot_f32(ah, bh) + (dot_f32(ah, bl) + dot_f32(al, bh))


def matern(dx, dy, rate2):
    t = (dx * dx + dy * dy) * rate2
    s = t * lax.rsqrt(jnp.maximum(t, 1e-30))
    return (1.0 + s) * jnp.exp(-s)


def tree_sum(xs):
    while len(xs) > 1:
        xs = [xs[i] + xs[i + 1] if i + 1 < len(xs) else xs[i] for i in range(0, len(xs), 2)]
    return xs[0]


def factor_block(rows):
    sub = lax.broadcasted_iota(jnp.int32, (SUB, NB), 0)
    lane = lax.broadcasted_iota(jnp.int32, (SUB, NB), 1)
    units = [(sub == k).astype(jnp.float32) for k in range(SUB)]
    groups = len(rows)
    r_all = list(rows)
    w_all = [(lane == sub + SUB * t).astype(jnp.float32) for t in range(groups)]
    out = []
    logs = jnp.zeros((SUB, NB), jnp.float32)
    for s in range(groups):
        r, w = r_all[s], w_all[s]
        cols = [lane_bcast(r, SUB * s + k) for k in range(SUB)]
        w_out = jnp.zeros((SUB, NB), jnp.float32)
        prod = None
        for k in range(SUB):
            d = row_bcast(cols[k], k)
            inv = 1.0 / d
            rs = lax.rsqrt(d)
            prod = d if prod is None else prod * d
            f = cols[k] - units[k]
            for m in range(k + 1, SUB):
                cols[m] = cols[m] - (f * row_bcast(cols[m], k)) * inv
            wk = row_bcast(w, k)
            w_out = jnp.where(sub == k, wk * rs, w_out)
            r = r - (f * row_bcast(r, k)) * inv
            w = w - (f * wk) * inv
        logs = logs + jnp.log(prod)
        out.append(w_out)
        if s + 1 < groups:
            r_rows = [row_bcast(r, k) for k in range(SUB)]
            w_rows = [row_bcast(w, k) for k in range(SUB)]
            for t in range(s + 1, groups):
                g = [lane_bcast(r_all[t], SUB * s + k) for k in range(SUB)]
                r_all[t] = r_all[t] - tree_sum([g[k] * r_rows[k] for k in range(SUB)])
                w_all[t] = w_all[t] - tree_sum([g[k] * w_rows[k] for k in range(SUB)])
    return out, logs


def kernel(
    tile, ls_ref, ng_ref, lead_ref, loc_ref, obs_ref,
    slab_ref, white_ref, ll_ref,
    a_ref, w_ref, y_ref, site_ref, row_ref, chi_ref, clo_ref, p1_ref, p2_ref, p3_ref,
):
    f32 = jnp.float32
    n_lead = 2 * tile
    nblk = n_lead // NB
    rows_total = loc_ref.shape[1]
    row_rank = lax.axis_index("prow")
    col_rank = lax.axis_index("pcol")
    row_procs = lax.axis_size("prow")
    ls = jnp.full((SUB, NB), ls_ref[0], f32)
    rate2 = 3.0 / (ls * ls)
    nugget = ng_ref[0]
    col_off = col_rank * SLAB_DEV
    col_tile = 2 + col_off // tile
    col_lane = pl.multiple_of(lax.rem(col_off, tile), SLAB_DEV)
    cx = lead_ref[col_tile, 0:1, pl.ds(col_lane, SLAB_DEV)]
    cy = lead_ref[col_tile, 1:2, pl.ds(col_lane, SLAB_DEV)]
    sub = lax.broadcasted_iota(jnp.int32, (SUB, NB), 0)
    lane = lax.broadcasted_iota(jnp.int32, (SUB, NB), 1)

    for q in range(nblk):
        t, o = divmod(q * NB, tile)
        stacked = jnp.concatenate(
            [lead_ref[t, :, o : o + NB], jnp.zeros((NB - 3, NB), f32)], axis=0
        )
        site_ref[q * NB : (q + 1) * NB, :] = stacked.T

    def row_columns(q, c):
        o = pl.multiple_of(q * NB, NB)
        stacked = jnp.concatenate(
            [loc_ref[:, pl.ds(o, NB)], jnp.zeros((NB - 2, NB), f32)], axis=0
        )
        row_ref[pl.ds(o, NB), :] = stacked.T
        return c

    lax.fori_loop(0, rows_total // NB, row_columns, 0)

    for b in range(nblk):
        def cov_rows(g, c, b=b):
            o = pl.multiple_of(b * NB + g * SUB, SUB)
            v = site_ref[pl.ds(o, SUB), :]
            x, y, ob = lane_bcast(v, 0), lane_bcast(v, 1), lane_bcast(v, 2)
            for j in range(b, nblk):
                t, u = divmod(j * NB, tile)
                val = matern(
                    x - lead_ref[t, 0:1, u : u + NB], y - lead_ref[t, 1:2, u : u + NB], rate2
                )
                if j == b:
                    val = jnp.where(lane == sub + g * SUB, val + nugget, val)
                a_ref[pl.ds(o, SUB), j * NB : (j + 1) * NB] = val
            a_ref[pl.ds(o, SUB), n_lead : n_lead + NB] = matern(x - cx, y - cy, rate2)
            a_ref[pl.ds(o, SUB), n_lead + NB : n_lead + 2 * NB] = jnp.where(lane < 2, ob, 0.0)
            return c

        lax.fori_loop(0, NB // SUB, cov_rows, 0)

    chunk = rows_total // nblk
    width = n_lead + 2 * NB

    def step(b, logs):
        o = pl.multiple_of(b * NB, NB)
        rows = [
            a_ref[pl.ds(pl.multiple_of(b * NB + SUB * t, SUB), SUB), pl.ds(o, NB)]
            for t in range(NB // SUB)
        ]
        out, more = factor_block(rows)
        w = jnp.concatenate(out, axis=0)
        w_ref[pl.ds(o, NB), :] = w

        def cov_chunk(g, c):
            ro = pl.multiple_of(b * chunk + g * 16, 16)
            for j in range(nblk):
                t, u = divmod(j * NB, tile)
                vals = []
                for h in range(2):
                    v = row_ref[pl.ds(pl.multiple_of(ro + h * SUB, SUB), SUB), :]
                    vals.append(matern(
                        lane_bcast(v, 0) - lead_ref[t, 0:1, u : u + NB],
                        lane_bcast(v, 1) - lead_ref[t, 1:2, u : u + NB],
                        rate2,
                    ))
                hi, lo = split2(jnp.concatenate(vals, axis=0))
                chi_ref[pl.ds(ro, 16), j * NB : (j + 1) * NB] = hi
                clo_ref[pl.ds(ro, 16), j * NB : (j + 1) * NB] = lo
            return c

        lax.fori_loop(0, chunk // 16, cov_chunk, 0)

        for bb in range(nblk):
            @pl.when(b == bb)
            def _(bb=bb):
                r0, c0 = bb * NB, (bb + 1) * NB
                u = dot3(w, a_ref[r0 : r0 + NB, c0:width])
                a_ref[r0 : r0 + NB, c0:width] = u
                uh, ul = split2(u)
                for t in range(bb + 1, nblk):
                    lo = t * NB - c0
                    th = uh[:, lo : lo + NB].T
                    tl = ul[:, lo : lo + NB].T
                    rh, rl = uh[:, lo:], ul[:, lo:]
                    p = dot_f32(th, rh) + (dot_f32(th, rl) + dot_f32(tl, rh))
                    a_ref[t * NB : (t + 1) * NB, t * NB : width] -= p
        return logs + more

    logs = lax.fori_loop(0, nblk, step, jnp.zeros((SUB, NB), f32))

    for b in reversed(range(nblk)):
        r0, c0 = b * NB, (b + 1) * NB
        v = a_ref[r0:c0, n_lead:width]
        if b + 1 < nblk:
            v = v - dot3(a_ref[r0:c0, c0:n_lead], y_ref[c0:n_lead, :])
        y_ref[r0:c0, :] = dot3(w_ref[r0:c0, :].T, v)

    y = y_ref[...]
    yh, yl = split2(y)
    yt = ((y - yh.astype(f32)) - yl.astype(f32)).astype(jnp.bfloat16)
    first = lax.broadcasted_iota(jnp.int32, (n_lead, NB), 1) == 0
    p1_ref[...] = jnp.concatenate([yh[:, :NB], yl[:, :NB]], axis=1)
    obs_h, obs_l = yh[:, NB:].astype(f32), yl[:, NB:].astype(f32)
    p2_ref[...] = jnp.concatenate(
        [yt[:, :NB], jnp.where(first, obs_h, obs_l).astype(jnp.bfloat16)], axis=1
    )
    p3_ref[...] = jnp.concatenate(
        [yh[:, :NB], jnp.where(first, obs_h, 0.0).astype(jnp.bfloat16)], axis=1
    )

    z = a_ref[:, n_lead + NB : width]
    quad = 0.5 * jnp.sum(jnp.where(lax.broadcasted_iota(jnp.int32, z.shape, 1) == 0, z * z, 0.0), keepdims=True)
    ll_ref[...] = -(quad + 0.5 * logs[0:1, 0:1]) / float(n_lead)

    big = 2 * NB
    per_tile = tile // big

    for q in range(rows_total // big):
        o = q * big
        ch = chi_ref[o : o + big, :]
        acc = dot_f32(ch, p1_ref[...])
        acc2 = dot_f32(ch, p2_ref[...]) + dot_f32(clo_ref[o : o + big, :], p3_ref[...])
        corr = acc[:, :NB] + (acc[:, NB:] + acc2[:, :NB])
        t, off = divmod(o, tile)
        gid = (t * row_procs + row_rank) * tile + off
        leading = gid < n_lead
        v = row_ref[o : o + big, :]
        x = jnp.broadcast_to(v[:, 0:1], (big, NB))
        y = jnp.broadcast_to(v[:, 1:2], (big, NB))
        val = matern(x - cx, y - cy, rate2[0:1, :])
        rid = gid + lax.broadcasted_iota(jnp.int32, (big, NB), 0)
        cid = n_lead + col_off + lax.broadcasted_iota(jnp.int32, (big, NB), 1)
        val = jnp.where(rid == cid, val + nugget, val) - corr
        slab_ref[o : o + big, :] = jnp.where(leading, 0.0, val)
        for h in range(2):
            at = off + h * NB
            tr = acc2[h * NB : (h + 1) * NB, NB:].T
            rest = obs_ref[t : t + 1, at : at + NB] - (tr[0:1, :] + tr[1:2, :])
            if t == 0:
                zs = pl.multiple_of(jnp.where(leading, gid, 0) + h * NB, NB)
                zt = a_ref[pl.ds(zs, NB), n_lead + NB : width].T
                rest = jnp.where(leading, zt[0:1, :], rest)
            white_ref[t : t + 1, at : at + NB] = rest


def shards(coords, observations, length_scale, nugget):
    tile_count, tile = coords.shape[1:]
    rows = tile_count * tile
    n_lead = 2 * tile
    f32, bf16 = jnp.float32, jnp.bfloat16
    mine = jnp.concatenate([coords[:, 0, :], observations[0:1, :]], axis=0)
    lead = lax.all_gather(mine, "prow", axis=0)
    vmem = pl.BlockSpec(memory_space=pltpu.VMEM)
    smem = pl.BlockSpec(memory_space=pltpu.SMEM)
    slab, white, ll = pl.pallas_call(
        functools.partial(kernel, tile),
        out_shape=(
            jax.ShapeDtypeStruct((rows, SLAB_DEV), f32),
            jax.ShapeDtypeStruct((tile_count, tile), f32),
            jax.ShapeDtypeStruct((1, 1), f32),
        ),
        in_specs=[smem, smem, vmem, vmem, vmem],
        out_specs=(vmem, vmem, vmem),
        scratch_shapes=[
            pltpu.VMEM((n_lead, n_lead + 2 * NB), f32),
            pltpu.VMEM((n_lead, NB), f32),
            pltpu.VMEM((n_lead, 2 * NB), f32),
            pltpu.VMEM((n_lead, NB), f32),
            pltpu.VMEM((rows, NB), f32),
            pltpu.VMEM((rows, n_lead), bf16),
            pltpu.VMEM((rows, n_lead), bf16),
            pltpu.VMEM((n_lead, 2 * NB), bf16),
            pltpu.VMEM((n_lead, 2 * NB), bf16),
            pltpu.VMEM((n_lead, 2 * NB), bf16),
        ],
        compiler_params=pltpu.CompilerParams(vmem_limit_bytes=48 * 1024 * 1024),
    )(length_scale, nugget, lead, coords.reshape(2, rows), observations)
    return slab.reshape(tile_count, tile, SLAB_DEV), white, ll.reshape(1)


def solution(mesh):
    placed = (P(None, None, "prow"), P(None, "prow"), P(), P())
    return jax.shard_map(
        shards,
        mesh=mesh,
        in_specs=placed,
        out_specs=(P(None, "prow", "pcol"), P(None, "prow"), P()),
        check_vma=False,
    )
```

time: 508 us -> 114 us (0.22); the launches traced: 497 us -> 114 us
  other arithmetic: 250 us -> 0.01 us
  Pallas kernels: 0 us -> 103 us
  matrix products: 84.1 us -> 0 us
  local copies, waits for them, and re-layouts: 57.2 us -> 2.98 us
  waiting for transfers between devices: 40.8 us -> 0 us
  blocking collectives: 38.7 us -> 6.2 us
  between operations: 25.9 us -> 1.94 us
    another operation x34 -> x0, other arithmetic: 244 us -> none  [the longest x5 83.6 us: inverse_lower(): return jax.scipy.linalg.solve_triangular(factor, identity, lower=True)]
    pallas_call x0 -> x1, Pallas kernels: none -> 103 us  [shards(): pl.pallas_call(functools.partial(kernel, tile), out_shape=(jax.ShapeDtype...]
    dot_general x15 -> x0, matrix products: 62.1 us -> none  [the longest x10 55.6 us: transposed_product(): jnp.dot(left, right.T, precision=lax.Precision.HIGHEST, preferred_element...]
    all_gather x2 -> x0, waiting for transfers between devices: 40.7 us -> none  [the longest x1 40.7 us: shards(): lax.all_gather(share_second, 'pcol', axis=0, tiled=True)]
    all_gather x3 -> x1, blocking collectives: 38.7 us -> 6.2 us  [shards(): lead = lax.all_gather(mine, 'prow', axis=0)]
    gather x10 -> x0, local copies, waits for them, and re-layouts: 26.7 us -> none  [the longest x3 6.3 us: compute_second(): inside = jnp.take(factor_second, rows_ids % block_size, axis=0)]
    another operation x35 -> x0, local copies, waits for them, and re-layouts: 23 us -> none  [the longest x27 22.7 us: inverse_lower(): return jax.scipy.linalg.solve_triangular(factor, identity, lower=True)]
    another operation x26 -> x0, matrix products: 21.9 us -> none  [the longest x14 14.6 us: inverse_lower(): return jax.scipy.linalg.solve_triangular(factor, identity, lower=True)]
  transfers between devices with their start and end apart: 2 -> 0, of which waited for: 1 -> 0; matrix products, arithmetic and copies ran while one was open for 44% -> 0% of each run, Pallas kernels for 0% -> 0%
where the time goes in v1:
time: 114 us
  Pallas kernels  103 us (90%)
  blocking collectives  6.2 us (5%)
  local copies, waits for them, and re-layouts  2.98 us (3%)
  between operations  1.94 us (2%)
    pallas_call x1, Pallas kernels, shards(): pl.pallas_call(functools.partial(kernel, tile), out_shape=(jax.ShapeDtype...  103 us
    all_gather x1, blocking collectives, shards(): lead = lax.all_gather(mine, 'prow', axis=0)  6.2 us

profile of v1, /device:TPU:0, one launch (start us, length us, event | category | flops | bytes accessed | tf_op | source)
XLA Modules:
  0.0 113.8 jit_solution(7566864119136185912)
XLA Ops:
  1.9 0.7 slice.7
  2.6 0.8 slice.6
  3.4 6.2 %all-gather.1.lead_ref = f32[4,3,512]{2,1,0:T(4,128)S(1)} all-gather(f32[1,3,512]{2,1,0:T(4,128)S(1)} %maximum_bitcast_fusion), channel_id=2, replica_groups=mesh['prow'=4,'pcol'=8] {'prow'}, dimensions={0}, use_global_device_ids=true | all-gather | bytes 30720 | tf_op jit(solution)/shard_map/all_gather | solution.py:259
  9.6 0.8 copy.10
  10.4 0.0 copy-start
  10.4 0.7 copy-done
  11.1 102.7 %shard_map.67 = (f32[4096,128]{1,0:T(8,128)}, f32[8,512]{1,0:T(8,128)}, f32[1,1]{1,0:T(1,128)}) custom-call(f32[1]{0:T(128)S(6)} %copy.13.ls_ref, f32[1]{0:T(128)S(6)} %copy.14.ng_ref, f32[4,3,512]{2,1,0:T(4,128)S(1)} %all-gather.1.lead_ref, f32[2,4096]{1,0:T(2,128)S(1)} %bitcast.9, f32[8,512]{1,0:T(8,128)S(1)} %copy-done), custom_call_target="tpu_custom_call" | custom-call | tf_op jit(solution)/shard_map/pallas_call | solution.py:262
  (2 shorter events, 0.0 us)
Async XLA Ops:
  10.4 0.7 copy-start

commit v2 on v1

--- a/solution.py
+++ b/solution.py
@@ -36,10 +36,14 @@
     return dot_f32(ah, bh) + (dot_f32(ah, bl) + dot_f32(al, bh))
 
 
+LOG2E = 1.4426950408889634
+
+
 def matern(dx, dy, rate2):
     t = (dx * dx + dy * dy) * rate2
     s = t * lax.rsqrt(jnp.maximum(t, 1e-30))
-    return (1.0 + s) * jnp.exp(-s)
+    e = jnp.exp2(s * -LOG2E)
+    return e + s * e
 
 
 def tree_sum(xs):
@@ -48,7 +52,7 @@
     return xs[0]
 
 
-def factor_block(rows):
+def factor_block(rows, fill):
     sub = lax.broadcasted_iota(jnp.int32, (SUB, NB), 0)
     lane = lax.broadcasted_iota(jnp.int32, (SUB, NB), 1)
     units = [(sub == k).astype(jnp.float32) for k in range(SUB)]
@@ -57,32 +61,48 @@
     w_all = [(lane == sub + SUB * t).astype(jnp.float32) for t in range(groups)]
     out = []
     logs = jnp.zeros((SUB, NB), jnp.float32)
+    cols = [lane_bcast(r_all[0], k) for k in range(SUB)]
     for s in range(groups):
         r, w = r_all[s], w_all[s]
-        cols = [lane_bcast(r, SUB * s + k) for k in range(SUB)]
+        more = s + 1 < groups
+        if more:
+            g_next = [lane_bcast(r_all[s + 1], SUB * s + k) for k in range(SUB)]
+            low = list(g_next)
+            ahead = [lane_bcast(r_all[s + 1], SUB * (s + 1) + k) for k in range(SUB)]
         w_out = jnp.zeros((SUB, NB), jnp.float32)
         prod = None
         for k in range(SUB):
             d = row_bcast(cols[k], k)
-            inv = 1.0 / d
+            inv = pltpu.reciprocal(d, approx=True)
             rs = lax.rsqrt(d)
             prod = d if prod is None else prod * d
             f = cols[k] - units[k]
             for m in range(k + 1, SUB):
-                cols[m] = cols[m] - (f * row_bcast(cols[m], k)) * inv
+                e = row_bcast(cols[m], k)
+                cols[m] = cols[m] - (f * e) * inv
+                if more:
+                    low[m] = low[m] - low[k] * (e * inv)
+            if more:
+                h = low[k] * inv
+                for m in range(SUB):
+                    ahead[m] = ahead[m] - h * row_bcast(low[k], m)
             wk = row_bcast(w, k)
             w_out = jnp.where(sub == k, wk * rs, w_out)
             r = r - (f * row_bcast(r, k)) * inv
             w = w - (f * wk) * inv
+            fill(s, k)
         logs = logs + jnp.log(prod)
         out.append(w_out)
-        if s + 1 < groups:
+        if more:
             r_rows = [row_bcast(r, k) for k in range(SUB)]
             w_rows = [row_bcast(w, k) for k in range(SUB)]
             for t in range(s + 1, groups):
-                g = [lane_bcast(r_all[t], SUB * s + k) for k in range(SUB)]
+                g = g_next if t == s + 1 else [
+                    lane_bcast(r_all[t], SUB * s + k) for k in range(SUB)
+                ]
                 r_all[t] = r_all[t] - tree_sum([g[k] * r_rows[k] for k in range(SUB)])
                 w_all[t] = w_all[t] - tree_sum([g[k] * w_rows[k] for k in range(SUB)])
+            cols = ahead
     return out, logs
 
 
@@ -116,16 +136,6 @@
         )
         site_ref[q * NB : (q + 1) * NB, :] = stacked.T
 
-    def row_columns(q, c):
-        o = pl.multiple_of(q * NB, NB)
-        stacked = jnp.concatenate(
-            [loc_ref[:, pl.ds(o, NB)], jnp.zeros((NB - 2, NB), f32)], axis=0
-        )
-        row_ref[pl.ds(o, NB), :] = stacked.T
-        return c
-
-    lax.fori_loop(0, rows_total // NB, row_columns, 0)
-
     for b in range(nblk):
         def cov_rows(g, c, b=b):
             o = pl.multiple_of(b * NB + g * SUB, SUB)
@@ -143,7 +153,7 @@
             a_ref[pl.ds(o, SUB), n_lead + NB : n_lead + 2 * NB] = jnp.where(lane < 2, ob, 0.0)
             return c
 
-        lax.fori_loop(0, NB // SUB, cov_rows, 0)
+        lax.fori_loop(0, NB // SUB, cov_rows, 0, unroll=4)
 
     chunk = rows_total // nblk
     width = n_lead + 2 * NB
@@ -154,28 +164,41 @@
             a_ref[pl.ds(pl.multiple_of(b * NB + SUB * t, SUB), SUB), pl.ds(o, NB)]
             for t in range(NB // SUB)
         ]
-        out, more = factor_block(rows)
-        w = jnp.concatenate(out, axis=0)
-        w_ref[pl.ds(o, NB), :] = w
-
-        def cov_chunk(g, c):
-            ro = pl.multiple_of(b * chunk + g * 16, 16)
-            for j in range(nblk):
+        for q in range(chunk // NB):
+            at = pl.multiple_of(b * chunk + q * NB, NB)
+            stacked = jnp.concatenate(
+                [loc_ref[:, pl.ds(at, NB)], jnp.zeros((NB - 2, NB), f32)], axis=0
+            )
+            row_ref[pl.ds(at, NB), :] = stacked.T
+
+        per_group = chunk // (NB // SUB)
+        units_total = (per_group // 16) * nblk
+        held = {}
+
+        def fill(s, k):
+            for unit in range(k * units_total // SUB, (k + 1) * units_total // SUB):
+                pair, j = divmod(unit, nblk)
+                ro = pl.multiple_of(b * chunk + s * per_group + pair * 16, 16)
+                if j == 0:
+                    for h in range(2):
+                        v = row_ref[pl.ds(pl.multiple_of(ro + h * SUB, SUB), SUB), :]
+                        held[h] = lane_bcast(v, 0), lane_bcast(v, 1)
                 t, u = divmod(j * NB, tile)
-                vals = []
-                for h in range(2):
-                    v = row_ref[pl.ds(pl.multiple_of(ro + h * SUB, SUB), SUB), :]
-                    vals.append(matern(
-                        lane_bcast(v, 0) - lead_ref[t, 0:1, u : u + NB],
-                        lane_bcast(v, 1) - lead_ref[t, 1:2, u : u + NB],
+                vals = [
+                    matern(
+                        held[h][0] - lead_ref[t, 0:1, u : u + NB],
+                        held[h][1] - lead_ref[t, 1:2, u : u + NB],
                         rate2,
-                    ))
+                    )
+                    for h in range(2)
+                ]
                 hi, lo = split2(jnp.concatenate(vals, axis=0))
                 chi_ref[pl.ds(ro, 16), j * NB : (j + 1) * NB] = hi
                 clo_ref[pl.ds(ro, 16), j * NB : (j + 1) * NB] = lo
-            return c
-
-        lax.fori_loop(0, chunk // 16, cov_chunk, 0)
+
+        out, more = factor_block(rows, fill)
+        w = jnp.concatenate(out, axis=0)
+        w_ref[pl.ds(o, NB), :] = w
 
         for bb in range(nblk):
             @pl.when(b == bb)

time: 114 us -> 69.2 us (0.61)
  Pallas kernels: 103 us -> 57.7 us
    pallas_call x1, Pallas kernels: 103 us -> 57.7 us  [shards(): pl.pallas_call(functools.partial(kernel, tile), out_shape=(jax.ShapeDtype...]
where the time goes in v2:
time: 69.2 us; the launch traced here: 68.8 us
  Pallas kernels  57.7 us (83%)
  blocking collectives  6.2 us (9%)
  local copies, waits for them, and re-layouts  2.98 us (4%)
  between operations  1.94 us (3%)
    pallas_call x1, Pallas kernels, shards(): pl.pallas_call(functools.partial(kernel, tile), out_shape=(jax.ShapeDtype...  57.7 us
    all_gather x1, blocking collectives, shards(): lead = lax.all_gather(mine, 'prow', axis=0)  6.2 us
    unnamed x4, local copies, waits for them, and re-layouts  1.5 us
    slice x2, local copies, waits for them, and re-layouts, shards(): mine = jnp.concatenate([coords[:, 0, :], observations[0:1, :]], axis=0)  1.48 us

profile of v2, /device:TPU:0, one launch (start us, length us, event | category | flops | bytes accessed | tf_op | source)
XLA Modules:
  0.0 68.8 jit_solution(2662209032702040358)
XLA Ops:
  1.9 0.7 %slice.7 = f32[1,512]{1,0:T(1,128)S(1)} slice(f32[8,512]{1,0:T(8,128)} %obs_ref.1), slice={[0:1], [0:512]} | slice | bytes 4096 | tf_op jit(solution)/shard_map/slice | solution.py:281
  2.6 0.8 %slice.6 = f32[2,1,512]{2,1,0:T(1,128)S(1)} slice(f32[2,8,512]{2,1,0:T(8,128)} %param.4), slice={[0:2], [0:1], [0:512]} | slice | bytes 8192 | tf_op jit(solution)/shard_map/slice | solution.py:281
  3.4 6.2 %all-gather.1.lead_ref = f32[4,3,512]{2,1,0:T(4,128)S(1)} all-gather(f32[1,3,512]{2,1,0:T(4,128)S(1)} %maximum_bitcast_fusion), channel_id=2, replica_groups=mesh['prow'=4,'pcol'=8] {'prow'}, dimensions={0}, use_global_device_ids=true | all-gather | bytes 30720 | tf_op jit(solution)/shard_map/all_gather | solution.py:282
  9.6 0.8 %copy.10 = f32[1,2,8,512]{3,1,2,0:T(2,128)S(1)} copy(f32[1,2,8,512]{3,2,1,0:T(8,128)} %bitcast.10) | data formatting | bytes 65536
  10.4 0.0 copy-start
  10.4 0.7 %copy-done = f32[8,512]{1,0:T(8,128)S(1)} copy-done((f32[8,512]{1,0:T(8,128)S(1)}, f32[8,512]{1,0:T(8,128)}, u32[]{:S(2)}) %copy-start) | copy-done | bytes 16408
  11.1 57.7 %shard_map.67 = (f32[4096,128]{1,0:T(8,128)}, f32[8,512]{1,0:T(8,128)}, f32[1,1]{1,0:T(1,128)}) custom-call(f32[1]{0:T(128)S(6)} %copy.13.ls_ref, f32[1]{0:T(128)S(6)} %copy.14.ng_ref, f32[4,3,512]{2,1,0:T(4,128)S(1)} %all-gather.1.lead_ref, f32[2,4096]{1,0:T(2,128)S(1)} %bitcast.9, f32[8,512]{1,0:T(8,128)S(1)} %copy-done), custom_call_target="tpu_custom_call" | custom-call | tf_op jit(solution)/shard_map/pallas_call | solution.py:285
  (2 shorter events, 0.0 us)
Async XLA Ops:
  10.4 0.7 %copy-start = (f32[8,512]{1,0:T(8,128)S(1)}, f32[8,512]{1,0:T(8,128)}, u32[]{:S(2)}) copy-start(f32[8,512]{1,0:T(8,128)} %obs_ref.1) | copy-start | bytes 49156

commit v3 on v2

v3 whole, which is shorter than its diff:
```python
import functools

import jax
import jax.numpy as jnp
from jax import lax
from jax.experimental import pallas as pl
from jax.experimental.pallas import tpu as pltpu
from jax.sharding import PartitionSpec as P

SLAB_DEV = 128
NB = 128
SUB = 8


def lane_bcast(v, c):
    return jnp.broadcast_to(v[:, c : c + 1], v.shape)


def row_bcast(v, k):
    return jnp.broadcast_to(v[k : k + 1, :], v.shape)


def split2(x):
    hi = x.astype(jnp.bfloat16)
    lo = (x - hi.astype(jnp.float32)).astype(jnp.bfloat16)
    return hi, lo


def dot_f32(a, b):
    return jnp.dot(a, b, preferred_element_type=jnp.float32)


LOG2E = 1.4426950408889634


def matern(dx, dy, rate2):
    t = (dx * dx + dy * dy) * rate2
    s = t * lax.rsqrt(jnp.maximum(t, 1e-30))
    e = jnp.exp2(s * -LOG2E)
    return e + s * e


def tree_sum(xs):
    while len(xs) > 1:
        xs = [xs[i] + xs[i + 1] if i + 1 < len(xs) else xs[i] for i in range(0, len(xs), 2)]
    return xs[0]


def factor_block(rows, fill):
    sub = lax.broadcasted_iota(jnp.int32, (SUB, NB), 0)
    lane = lax.broadcasted_iota(jnp.int32, (SUB, NB), 1)
    units = [(sub == k).astype(jnp.float32) for k in range(SUB)]
    groups = len(rows)
    r_all = list(rows)
    w_all = [(lane == sub + SUB * t).astype(jnp.float32) for t in range(groups)]
    out = []
    logs = jnp.zeros((SUB, NB), jnp.float32)
    cols = [lane_bcast(r_all[0], k) for k in range(SUB)]
    for s in range(groups):
        r, w = r_all[s], w_all[s]
        more = s + 1 < groups
        if more:
            g_next = [lane_bcast(r_all[s + 1], SUB * s + k) for k in range(SUB)]
            low = list(g_next)
            ahead = [lane_bcast(r_all[s + 1], SUB * (s + 1) + k) for k in range(SUB)]
        w_out = jnp.zeros((SUB, NB), jnp.float32)
        prod = None
        for k in range(SUB):
            d = row_bcast(cols[k], k)
            inv = pltpu.reciprocal(d, approx=True)
            rs = lax.rsqrt(d)
            prod = d if prod is None else prod * d
            f = cols[k] - units[k]
            fi = f * inv
            h = low[k] * inv if more else None
            for m in range(k + 1, SUB):
                e = row_bcast(cols[m], k)
                cols[m] = cols[m] - ((f * e) * inv if m == k + 1 else fi * e)
                if more:
                    low[m] = low[m] - h * e
            if more:
                for m in range(SUB):
                    ahead[m] = ahead[m] - h * row_bcast(low[k], m)
            wk = row_bcast(w, k)
            w_out = jnp.where(sub == k, wk * rs, w_out)
            r = r - fi * row_bcast(r, k)
            w = w - fi * wk
            fill(s, k)
        logs = logs + jnp.log(prod)
        out.append(w_out)
        if more:
            r_rows = [row_bcast(r, k) for k in range(SUB)]
            w_rows = [row_bcast(w, k) for k in range(SUB)]
            for t in range(s + 1, groups):
                g = g_next if t == s + 1 else [
                    lane_bcast(r_all[t], SUB * s + k) for k in range(SUB)
                ]
                r_all[t] = r_all[t] - tree_sum([g[k] * r_rows[k] for k in range(SUB)])
                w_all[t] = w_all[t] - tree_sum([g[k] * w_rows[k] for k in range(SUB)])
            cols = ahead
    return out, logs


def kernel(
    tile, ls_ref, ng_ref, lead_ref, loc_ref, obs_ref,
    slab_ref, white_ref, ll_ref,
    a_ref, z_ref, site_ref, row_ref, chi_ref, clo_ref, p1_ref, p2_ref, p3_ref,
    d_ref, winv_ref, pinv_ref, col_ref, mh_ref, ml_ref,
):
    f32, bf16 = jnp.float32, jnp.bfloat16
    n_lead = 2 * tile
    nblk = n_lead // NB
    width = n_lead + 2 * NB
    rows_total = loc_ref.shape[1]
    row_rank = lax.axis_index("prow")
    col_rank = lax.axis_index("pcol")
    row_procs = lax.axis_size("prow")
    ls = jnp.full((SUB, NB), ls_ref[0], f32)
    rate2 = 3.0 / (ls * ls)
    nugget = ng_ref[0]
    col_off = col_rank * SLAB_DEV
    col_tile = 2 + col_off // tile
    col_lane = pl.multiple_of(lax.rem(col_off, tile), SLAB_DEV)
    cx = lead_ref[col_tile, 0:1, pl.ds(col_lane, SLAB_DEV)]
    cy = lead_ref[col_tile, 1:2, pl.ds(col_lane, SLAB_DEV)]
    sub = lax.broadcasted_iota(jnp.int32, (SUB, NB), 0)
    lane = lax.broadcasted_iota(jnp.int32, (SUB, NB), 1)

    def columns(coord):
        pad = jnp.zeros((NB - coord.shape[0], NB), f32)
        return jnp.concatenate([coord, pad], axis=0).T

    def site_columns(q):
        t, o = divmod(q * NB, tile)
        site_ref[q * NB : (q + 1) * NB, :] = columns(lead_ref[t, :, o : o + NB])

    def row_columns(q):
        row_ref[q * NB : (q + 1) * NB, :] = columns(loc_ref[:, q * NB : (q + 1) * NB])

    held = {}

    def cov_piece(b, g, j):
        o = b * NB + g * SUB
        if ("site", o) not in held:
            v = site_ref[o : o + SUB, :]
            held["site", o] = [lane_bcast(v, c) for c in range(3)]
        x, y, ob = held["site", o]
        if j < nblk:
            t, u = divmod(j * NB, tile)
            val = matern(x - lead_ref[t, 0:1, u : u + NB], y - lead_ref[t, 1:2, u : u + NB], rate2)
            if j == b:
                val = jnp.where(lane == sub + g * SUB, val + nugget, val)
        elif j == nblk:
            val = matern(x - cx, y - cy, rate2)
        else:
            val = jnp.where(lane < 2, ob, 0.0)
        a_ref[o : o + SUB, j * NB : (j + 1) * NB] = val

    def row_piece(ro, key, j):
        if key not in held:
            held[key] = []
            for h in range(2):
                v = row_ref[pl.ds(pl.multiple_of(ro + h * SUB, SUB), SUB), :]
                held[key].append((lane_bcast(v, 0), lane_bcast(v, 1)))
        t, u = divmod(j * NB, tile)
        vals = [
            matern(x - lead_ref[t, 0:1, u : u + NB], y - lead_ref[t, 1:2, u : u + NB], rate2)
            for x, y in held[key]
        ]
        hi, lo = split2(jnp.concatenate(vals, axis=0))
        chi_ref[pl.ds(ro, 16), j * NB : (j + 1) * NB] = hi
        clo_ref[pl.ds(ro, 16), j * NB : (j + 1) * NB] = lo

    def three(al_parts, bh, bl):
        depth = bh.shape[0]
        return dot_f32(al_parts, jnp.concatenate([bh, bh], axis=0)) + dot_f32(
            al_parts[:, :depth], bl
        )

    def parts(x):
        return jnp.concatenate(split2(x), axis=1)

    def multiplier_piece(j0, j1):
        m = three(pinv_ref[...], *split2(a_ref[0:NB, j0:j1]))
        mh_ref[:, j0:j1], ml_ref[:, j0:j1] = split2(m)
        return m

    def column_parts():
        col_ref[...] = parts(a_ref[NB:n_lead, 0:NB])

    def update_piece(j0, j1, r0, r1, shift):
        new = a_ref[r0:r1, j0:j1] - three(
            col_ref[r0 - NB : r1 - NB, :], mh_ref[:, j0:j1], ml_ref[:, j0:j1]
        )
        a_ref[r0 - NB : r1 - NB, j0 - shift : j1 - shift] = new

    def tile_pieces(j0, j1, shift):
        box = {}

        def first():
            box["m"] = multiplier_piece(j0, j1)

        def last():
            a_ref[n_lead - NB : n_lead, j0 - shift : j1 - shift] = box["m"]

        half = (nblk // 2 + 1) * NB
        return [
            first,
            functools.partial(update_piece, j0, j1, NB, half, shift),
            functools.partial(update_piece, j0, j1, half, n_lead, shift),
            last,
        ]

    def keep_z(at):
        z_ref[pl.ds(at, NB), :] = three(
            winv_ref[...], *split2(a_ref[0:NB, n_lead + NB : width])
        )

    def finish_block(out, more_blocks):
        w = jnp.concatenate(out, axis=0)
        wt = w.T
        w_parts = parts(w)
        winv_ref[...] = w_parts
        wh, wl = w_parts[:, :NB], w_parts[:, NB:]
        if more_blocks:
            u = three(w_parts, *split2(a_ref[0:NB, NB : 2 * NB]))
            ut = three(parts(a_ref[NB : 2 * NB, 0:NB]), *split2(wt))
            d_ref[...] = a_ref[NB : 2 * NB, NB : 2 * NB] - three(parts(ut), *split2(u))
        pinv_ref[...] = parts(three(parts(wt), wh, wl))

    def load_rows():
        return [d_ref[SUB * t : SUB * (t + 1), :] for t in range(NB // SUB)]

    slots = (NB // SUB) * SUB

    def planned(urgent, work):
        plan = [[] for _ in range(slots)]
        early = slots * 7 // 8
        for i, f in enumerate(urgent):
            plan[i * early // len(urgent)].append(f)
        for i, f in enumerate(work):
            plan[i * slots // len(work)].append(f)

        def fill(s, k):
            for f in plan[s * SUB + k]:
                f()

        return fill

    for q in range(nblk):
        site_columns(q)
    for g in range(NB // SUB):
        cov_piece(0, g, 0)
    d_ref[...] = a_ref[0:NB, 0:NB]
    work = [
        functools.partial(cov_piece, b, g, j)
        for b in range(nblk)
        for g in range(NB // SUB)
        for j in range(nblk + 2)
        if (b, j) != (0, 0)
    ]
    urgent = [functools.partial(row_columns, q) for q in range(rows_total // NB)]
    out, logs = factor_block(load_rows(), planned(urgent, work))
    finish_block(out, True)

    chunk = -(-rows_total // 16 // (nblk - 1)) * 16
    col_tiles = [(j * NB, min(j + 2, nblk) * NB) for j in range(1, nblk, 2)]

    def step(b, logs):
        held.clear()
        base = jnp.minimum((b - 1) * chunk, rows_total - chunk)
        work = [
            functools.partial(
                row_piece, pl.multiple_of(base + pair * 16, 16), ("row", pair), j
            )
            for pair in range(chunk // 16)
            for j in range(nblk)
        ]
        urgent = [column_parts]
        for j0, j1 in col_tiles:
            urgent += tile_pieces(j0, j1, NB)
        urgent += [functools.partial(keep_z, pl.multiple_of((b - 1) * NB, NB))]
        urgent += tile_pieces(n_lead, width, 0)
        out, more = factor_block(load_rows(), planned(urgent, work))
        finish_block(out, True)
        return logs + more

    logs = lax.fori_loop(1, nblk, step, logs)
    column_parts()
    keep_z(n_lead - NB)
    for f in tile_pieces(n_lead, width, 0):
        f()

    y = a_ref[:, n_lead:width]
    yh, yl = split2(y)
    yt = ((y - yh.astype(f32)) - yl.astype(f32)).astype(bf16)
    first = lax.broadcasted_iota(jnp.int32, (n_lead, NB), 1) == 0
    p1_ref[...] = jnp.concatenate([yh[:, :NB], yl[:, :NB]], axis=1)
    obs_h, obs_l = yh[:, NB:].astype(f32), yl[:, NB:].astype(f32)
    p2_ref[...] = jnp.concatenate(
        [yt[:, :NB], jnp.where(first, obs_h, obs_l).astype(bf16)], axis=1
    )
    p3_ref[...] = jnp.concatenate(
        [yh[:, :NB], jnp.where(first, obs_h, 0.0).astype(bf16)], axis=1
    )

    z = z_ref[...]
    quad = 0.5 * jnp.sum(jnp.where(first, z * z, 0.0), keepdims=True)
    ll_ref[...] = -(quad + 0.5 * logs[0:1, 0:1]) / float(n_lead)

    big = 2 * NB
    for q in range(rows_total // big):
        o = q * big
        ch = chi_ref[o : o + big, :]
        acc = dot_f32(ch, p1_ref[...])
        acc2 = dot_f32(ch, p2_ref[...]) + dot_f32(clo_ref[o : o + big, :], p3_ref[...])
        corr = acc[:, :NB] + (acc[:, NB:] + acc2[:, :NB])
        t, off = divmod(o, tile)
        gid = (t * row_procs + row_rank) * tile + off
        leading = gid < n_lead
        v = row_ref[o : o + big, :]
        x = jnp.broadcast_to(v[:, 0:1], (big, NB))
        y = jnp.broadcast_to(v[:, 1:2], (big, NB))
        val = matern(x - cx, y - cy, rate2[0:1, :])
        rid = gid + lax.broadcasted_iota(jnp.int32, (big, NB), 0)
        cid = n_lead + col_off + lax.broadcasted_iota(jnp.int32, (big, NB), 1)
        val = jnp.where(rid == cid, val + nugget, val) - corr
        slab_ref[o : o + big, :] = jnp.where(leading, 0.0, val)
        for h in range(2):
            at = off + h * NB
            tr = acc2[h * NB : (h + 1) * NB, NB:].T
            rest = obs_ref[t : t + 1, at : at + NB] - (tr[0:1, :] + tr[1:2, :])
            if t == 0:
                zs = pl.multiple_of(jnp.where(leading, gid, 0) + h * NB, NB)
                zt = z_ref[pl.ds(zs, NB), :].T
                rest = jnp.where(leading, zt[0:1, :], rest)
            white_ref[t : t + 1, at : at + NB] = rest


def shards(coords, observations, length_scale, nugget):
    tile_count, tile = coords.shape[1:]
    rows = tile_count * tile
    n_lead = 2 * tile
    width = n_lead + 2 * NB
    f32, bf16 = jnp.float32, jnp.bfloat16
    mine = jnp.concatenate([coords[:, 0, :], observations[0:1, :]], axis=0)
    lead = lax.all_gather(mine, "prow", axis=0)
    vmem = pl.BlockSpec(memory_space=pltpu.VMEM)
    smem = pl.BlockSpec(memory_space=pltpu.SMEM)
    slab, white, ll = pl.pallas_call(
        functools.partial(kernel, tile),
        out_shape=(
            jax.ShapeDtypeStruct((rows, SLAB_DEV), f32),
            jax.ShapeDtypeStruct((tile_count, tile), f32),
            jax.ShapeDtypeStruct((1, 1), f32),
        ),
        in_specs=[smem, smem, vmem, vmem, vmem],
        out_specs=(vmem, vmem, vmem),
        scratch_shapes=[
            pltpu.VMEM((n_lead, width), f32),
            pltpu.VMEM((n_lead, NB), f32),
            pltpu.VMEM((n_lead, NB), f32),
            pltpu.VMEM((rows, NB), f32),
            pltpu.VMEM((rows, n_lead), bf16),
            pltpu.VMEM((rows, n_lead), bf16),
            pltpu.VMEM((n_lead, 2 * NB), bf16),
            pltpu.VMEM((n_lead, 2 * NB), bf16),
            pltpu.VMEM((n_lead, 2 * NB), bf16),
            pltpu.VMEM((NB, NB), f32),
            pltpu.VMEM((NB, 2 * NB), bf16),
            pltpu.VMEM((NB, 2 * NB), bf16),
            pltpu.VMEM((n_lead - NB, 2 * NB), bf16),
            pltpu.VMEM((NB, width), bf16),
            pltpu.VMEM((NB, width), bf16),
        ],
        compiler_params=pltpu.CompilerParams(vmem_limit_bytes=48 * 1024 * 1024),
    )(length_scale, nugget, lead, coords.reshape(2, rows), observations)
    return slab.reshape(tile_count, tile, SLAB_DEV), white, ll.reshape(1)


def solution(mesh):
    placed = (P(None, None, "prow"), P(None, "prow"), P(), P())
    return jax.shard_map(
        shards,
        mesh=mesh,
        in_specs=placed,
        out_specs=(P(None, "prow", "pcol"), P(None, "prow"), P()),
        check_vma=False,
    )
```

time: 69.2 us -> 61.6 us (0.89)
  Pallas kernels: 57.7 us -> 50.1 us
    pallas_call x1, Pallas kernels: 57.7 us -> 50.1 us  [shards(): pl.pallas_call(functools.partial(kernel, tile), out_shape=(jax.ShapeDtype...]
where the time goes in v3:
time: 61.6 us; the launch traced here: 61.3 us
  Pallas kernels  50.1 us (81%)
  blocking collectives  6.2 us (10%)
  local copies, waits for them, and re-layouts  2.98 us (5%)
  between operations  1.94 us (3%)
    pallas_call x1, Pallas kernels, shards(): pl.pallas_call(functools.partial(kernel, tile), out_shape=(jax.ShapeDtype...  50.1 us
    all_gather x1, blocking collectives, shards(): lead = lax.all_gather(mine, 'prow', axis=0)  6.2 us
    unnamed x4, local copies, waits for them, and re-layouts  1.5 us
    slice x2, local copies, waits for them, and re-layouts, shards(): mine = jnp.concatenate([coords[:, 0, :], observations[0:1, :]], axis=0)  1.48 us

profile of v3, /device:TPU:0, one launch (start us, length us, event | category | flops | bytes accessed | tf_op | source)
XLA Modules:
  0.0 61.3 jit_solution(10105674677535900381)
XLA Ops:
  1.9 0.7 %slice.7 = f32[1,512]{1,0:T(1,128)S(1)} slice(f32[8,512]{1,0:T(8,128)} %obs_ref.1), slice={[0:1], [0:512]} | slice | bytes 4096 | tf_op jit(solution)/shard_map/slice | solution.py:346
  2.6 0.8 %slice.6 = f32[2,1,512]{2,1,0:T(1,128)S(1)} slice(f32[2,8,512]{2,1,0:T(8,128)} %param.4), slice={[0:2], [0:1], [0:512]} | slice | bytes 8192 | tf_op jit(solution)/shard_map/slice | solution.py:346
  3.4 6.2 %all-gather.1.lead_ref = f32[4,3,512]{2,1,0:T(4,128)S(1)} all-gather(f32[1,3,512]{2,1,0:T(4,128)S(1)} %maximum_bitcast_fusion), channel_id=2, replica_groups=mesh['prow'=4,'pcol'=8] {'prow'}, dimensions={0}, use_global_device_ids=true | all-gather | bytes 30720 | tf_op jit(solution)/shard_map/all_gather | solution.py:347
  9.6 0.8 %copy.10 = f32[1,2,8,512]{3,1,2,0:T(2,128)S(1)} copy(f32[1,2,8,512]{3,2,1,0:T(8,128)} %bitcast.10) | data formatting | bytes 65536
  10.4 0.0 copy-start
  10.4 0.7 %copy-done = f32[8,512]{1,0:T(8,128)S(1)} copy-done((f32[8,512]{1,0:T(8,128)S(1)}, f32[8,512]{1,0:T(8,128)}, u32[]{:S(2)}) %copy-start) | copy-done | bytes 16408
  11.1 50.1 %shard_map.67 = (f32[4096,128]{1,0:T(8,128)}, f32[8,512]{1,0:T(8,128)}, f32[1,1]{1,0:T(1,128)}) custom-call(f32[1]{0:T(128)S(6)} %copy.13.ls_ref, f32[1]{0:T(128)S(6)} %copy.14.ng_ref, f32[4,3,512]{2,1,0:T(4,128)S(1)} %all-gather.1.lead_ref, f32[2,4096]{1,0:T(2,128)S(1)} %bitcast.9, f32[8,512]{1,0:T(8,128)S(1)} %copy-done), custom_call_target="tpu_custom_call" | custom-call | tf_op jit(solution)/shard_map/pallas_call | solution.py:350
  (2 shorter events, 0.0 us)
Async XLA Ops:
  10.4 0.7 %copy-start = (f32[8,512]{1,0:T(8,128)S(1)}, f32[8,512]{1,0:T(8,128)}, u32[]{:S(2)}) copy-start(f32[8,512]{1,0:T(8,128)} %obs_ref.1) | copy-start | bytes 49156

commit v4 on v3

--- a/solution.py
+++ b/solution.py
@@ -51,52 +51,58 @@
     lane = lax.broadcasted_iota(jnp.int32, (SUB, NB), 1)
     units = [(sub == k).astype(jnp.float32) for k in range(SUB)]
     groups = len(rows)
-    r_all = list(rows)
-    w_all = [(lane == sub + SUB * t).astype(jnp.float32) for t in range(groups)]
+    x_all = list(rows)
     out = []
     logs = jnp.zeros((SUB, NB), jnp.float32)
-    cols = [lane_bcast(r_all[0], k) for k in range(SUB)]
+    cols = [lane_bcast(x_all[0], k) for k in range(SUB)]
+    d = row_bcast(cols[0], 0)
     for s in range(groups):
-        r, w = r_all[s], w_all[s]
+        c0 = SUB * s
         more = s + 1 < groups
         if more:
-            g_next = [lane_bcast(r_all[s + 1], SUB * s + k) for k in range(SUB)]
+            g_next = [lane_bcast(x_all[s + 1], c0 + k) for k in range(SUB)]
             low = list(g_next)
-            ahead = [lane_bcast(r_all[s + 1], SUB * (s + 1) + k) for k in range(SUB)]
-        w_out = jnp.zeros((SUB, NB), jnp.float32)
+            ahead = [lane_bcast(x_all[s + 1], c0 + SUB + k) for k in range(SUB)]
+        here = (lane >= c0) & (lane < c0 + SUB)
+        x = jnp.where(here, (lane == sub + c0).astype(jnp.float32), x_all[s])
+        x_out = jnp.zeros((SUB, NB), jnp.float32)
         prod = None
         for k in range(SUB):
-            d = row_bcast(cols[k], k)
             inv = pltpu.reciprocal(d, approx=True)
             rs = lax.rsqrt(d)
             prod = d if prod is None else prod * d
+            if k + 1 < SUB:
+                e = row_bcast(cols[k + 1], k)
+                d = row_bcast(cols[k + 1], k + 1) - (e * e) * inv
+            elif more:
+                e = row_bcast(low[k], 0)
+                d = row_bcast(ahead[0], 0) - (e * e) * inv
             f = cols[k] - units[k]
             fi = f * inv
             h = low[k] * inv if more else None
             for m in range(k + 1, SUB):
                 e = row_bcast(cols[m], k)
-                cols[m] = cols[m] - ((f * e) * inv if m == k + 1 else fi * e)
+                cols[m] = cols[m] - ((f * e) * inv if m <= k + 2 else fi * e)
                 if more:
                     low[m] = low[m] - h * e
             if more:
                 for m in range(SUB):
                     ahead[m] = ahead[m] - h * row_bcast(low[k], m)
-            wk = row_bcast(w, k)
-            w_out = jnp.where(sub == k, wk * rs, w_out)
-            r = r - fi * row_bcast(r, k)
-            w = w - fi * wk
+            xk = row_bcast(x, k)
+            x_out = jnp.where(sub == k, xk * rs, x_out)
+            x = x - fi * xk
             fill(s, k)
         logs = logs + jnp.log(prod)
-        out.append(w_out)
+        out.append(jnp.where(lane < c0 + SUB, x_out, 0.0) if more else x_out)
         if more:
-            r_rows = [row_bcast(r, k) for k in range(SUB)]
-            w_rows = [row_bcast(w, k) for k in range(SUB)]
+            x_rows = [row_bcast(x, k) for k in range(SUB)]
             for t in range(s + 1, groups):
                 g = g_next if t == s + 1 else [
-                    lane_bcast(r_all[t], SUB * s + k) for k in range(SUB)
+                    lane_bcast(x_all[t], c0 + k) for k in range(SUB)
                 ]
-                r_all[t] = r_all[t] - tree_sum([g[k] * r_rows[k] for k in range(SUB)])
-                w_all[t] = w_all[t] - tree_sum([g[k] * w_rows[k] for k in range(SUB)])
+                x_all[t] = jnp.where(here, 0.0, x_all[t]) - tree_sum(
+                    [g[k] * x_rows[k] for k in range(SUB)]
+                )
             cols = ahead
     return out, logs
 

time: 61.6 us -> 59.5 us (0.966)
  Pallas kernels: 50.1 us -> 47.9 us
    pallas_call x1, Pallas kernels: 50.1 us -> 47.9 us  [shards(): pl.pallas_call(functools.partial(kernel, tile), out_shape=(jax.ShapeDtype...]
where the time goes in v4:
time: 59.5 us; the launch traced here: 59.1 us
  Pallas kernels  47.9 us (81%)
  blocking collectives  6.2 us (10%)
  local copies, waits for them, and re-layouts  2.98 us (5%)
  between operations  1.94 us (3%)
    pallas_call x1, Pallas kernels, shards(): pl.pallas_call(functools.partial(kernel, tile), out_shape=(jax.ShapeDtype...  47.9 us
    all_gather x1, blocking collectives, shards(): lead = lax.all_gather(mine, 'prow', axis=0)  6.2 us
    unnamed x4, local copies, waits for them, and re-layouts  1.5 us
    slice x2, local copies, waits for them, and re-layouts, shards(): mine = jnp.concatenate([coords[:, 0, :], observations[0:1, :]], axis=0)  1.48 us

profile of v4, /device:TPU:0, one launch (start us, length us, event | category | flops | bytes accessed | tf_op | source)
XLA Modules:
  0.0 59.1 jit_solution(12043535266651749784)
XLA Ops:
  1.9 0.7 %slice.7 = f32[1,512]{1,0:T(1,128)S(1)} slice(f32[8,512]{1,0:T(8,128)} %obs_ref.1), slice={[0:1], [0:512]} | slice | bytes 4096 | tf_op jit(solution)/shard_map/slice | solution.py:352
  2.6 0.8 %slice.6 = f32[2,1,512]{2,1,0:T(1,128)S(1)} slice(f32[2,8,512]{2,1,0:T(8,128)} %param.4), slice={[0:2], [0:1], [0:512]} | slice | bytes 8192 | tf_op jit(solution)/shard_map/slice | solution.py:352
  3.4 6.2 %all-gather.1.lead_ref = f32[4,3,512]{2,1,0:T(4,128)S(1)} all-gather(f32[1,3,512]{2,1,0:T(4,128)S(1)} %maximum_bitcast_fusion), channel_id=2, replica_groups=mesh['prow'=4,'pcol'=8] {'prow'}, dimensions={0}, use_global_device_ids=true | all-gather | bytes 30720 | tf_op jit(solution)/shard_map/all_gather | solution.py:353
  9.6 0.8 %copy.10 = f32[1,2,8,512]{3,1,2,0:T(2,128)S(1)} copy(f32[1,2,8,512]{3,2,1,0:T(8,128)} %bitcast.10) | data formatting | bytes 65536
  10.4 0.0 copy-start
  10.4 0.7 %copy-done = f32[8,512]{1,0:T(8,128)S(1)} copy-done((f32[8,512]{1,0:T(8,128)S(1)}, f32[8,512]{1,0:T(8,128)}, u32[]{:S(2)}) %copy-start) | copy-done | bytes 16408
  11.1 47.9 %shard_map.67 = (f32[4096,128]{1,0:T(8,128)}, f32[8,512]{1,0:T(8,128)}, f32[1,1]{1,0:T(1,128)}) custom-call(f32[1]{0:T(128)S(6)} %copy.13.ls_ref, f32[1]{0:T(128)S(6)} %copy.14.ng_ref, f32[4,3,512]{2,1,0:T(4,128)S(1)} %all-gather.1.lead_ref, f32[2,4096]{1,0:T(2,128)S(1)} %bitcast.9, f32[8,512]{1,0:T(8,128)S(1)} %copy-done), custom_call_target="tpu_custom_call" | custom-call | tf_op jit(solution)/shard_map/pallas_call | solution.py:356
  (2 shorter events, 0.0 us)
Async XLA Ops:
  10.4 0.7 %copy-start = (f32[8,512]{1,0:T(8,128)S(1)}, f32[8,512]{1,0:T(8,128)}, u32[]{:S(2)}) copy-start(f32[8,512]{1,0:T(8,128)} %obs_ref.1) | copy-start | bytes 49156

commit v5 on v4

--- a/solution.py
+++ b/solution.py
@@ -108,19 +108,33 @@
 
 
 def kernel(
-    tile, ls_ref, ng_ref, lead_ref, loc_ref, obs_ref,
-    slab_ref, white_ref, ll_ref,
-    a_ref, z_ref, site_ref, row_ref, chi_ref, clo_ref, p1_ref, p2_ref, p3_ref,
-    d_ref, winv_ref, pinv_ref, col_ref, mh_ref, ml_ref,
+    peers, ls_ref, ng_ref, loc_ref, obs_ref, *refs,
 ):
+    gathered, refs = refs[: max(2 * peers, 1)], refs[max(2 * peers, 1) :]
+    (
+        slab_ref, white_ref, ll_ref, lead_ref, a_ref, z_ref, site_ref, row_ref, chi_ref, clo_ref, p1_ref, p23_ref,
+        d_ref, winv_ref, pinv_ref, col_ref, mh_ref, ml_ref,
+    ) = refs
     f32, bf16 = jnp.float32, jnp.bfloat16
+    tile_count, tile = obs_ref.shape
     n_lead = 2 * tile
     nblk = n_lead // NB
     width = n_lead + 2 * NB
-    rows_total = loc_ref.shape[1]
+    rows_total = tile_count * tile
     row_rank = lax.axis_index("prow")
     col_rank = lax.axis_index("pcol")
     row_procs = lax.axis_size("prow")
+    if peers:
+        for t in range(peers + 1):
+            for c in range(3):
+                own = loc_ref[c, 0:1, :] if c < 2 else obs_ref[0:1, :]
+                for m in range(1, peers + 1):
+                    xy_ref, ob_ref = gathered[m - 1], gathered[peers + m - 1]
+                    theirs = xy_ref[c, 0:1, :] if c < 2 else ob_ref[0:1, :]
+                    own = jnp.where(row_rank == t ^ m, theirs, own)
+                lead_ref[t, c : c + 1, :] = own
+    else:
+        lead_ref[...] = gathered[0][...]
     ls = jnp.full((SUB, NB), ls_ref[0], f32)
     rate2 = 3.0 / (ls * ls)
     nugget = ng_ref[0]
@@ -141,7 +155,9 @@
         site_ref[q * NB : (q + 1) * NB, :] = columns(lead_ref[t, :, o : o + NB])
 
     def row_columns(q):
-        row_ref[q * NB : (q + 1) * NB, :] = columns(loc_ref[:, q * NB : (q + 1) * NB])
+        t, o = divmod(q * NB, tile)
+        here = [loc_ref[c, t : t + 1, o : o + NB] for c in range(2)]
+        row_ref[q * NB : (q + 1) * NB, :] = columns(jnp.concatenate(here, axis=0))
 
     held = {}
 
@@ -178,13 +194,11 @@
         clo_ref[pl.ds(ro, 16), j * NB : (j + 1) * NB] = lo
 
     def three(al_parts, bh, bl):
-        depth = bh.shape[0]
-        return dot_f32(al_parts, jnp.concatenate([bh, bh], axis=0)) + dot_f32(
-            al_parts[:, :depth], bl
-        )
+        return dot_f32(al_parts, jnp.concatenate([bh, bh, bl], axis=0))
 
     def parts(x):
-        return jnp.concatenate(split2(x), axis=1)
+        h, l = split2(x)
+        return jnp.concatenate([h, l, h], axis=1)
 
     def multiplier_piece(j0, j1):
         m = three(pinv_ref[...], *split2(a_ref[0:NB, j0:j1]))
@@ -227,7 +241,7 @@
         wt = w.T
         w_parts = parts(w)
         winv_ref[...] = w_parts
-        wh, wl = w_parts[:, :NB], w_parts[:, NB:]
+        wh, wl = w_parts[:, :NB], w_parts[:, NB : 2 * NB]
         if more_blocks:
             u = three(w_parts, *split2(a_ref[0:NB, NB : 2 * NB]))
             ut = three(parts(a_ref[NB : 2 * NB, 0:NB]), *split2(wt))
@@ -303,10 +317,10 @@
     first = lax.broadcasted_iota(jnp.int32, (n_lead, NB), 1) == 0
     p1_ref[...] = jnp.concatenate([yh[:, :NB], yl[:, :NB]], axis=1)
     obs_h, obs_l = yh[:, NB:].astype(f32), yl[:, NB:].astype(f32)
-    p2_ref[...] = jnp.concatenate(
+    p23_ref[0:n_lead, :] = jnp.concatenate(
         [yt[:, :NB], jnp.where(first, obs_h, obs_l).astype(bf16)], axis=1
     )
-    p3_ref[...] = jnp.concatenate(
+    p23_ref[n_lead : 2 * n_lead, :] = jnp.concatenate(
         [yh[:, :NB], jnp.where(first, obs_h, 0.0).astype(bf16)], axis=1
     )
 
@@ -314,12 +328,12 @@
     quad = 0.5 * jnp.sum(jnp.where(first, z * z, 0.0), keepdims=True)
     ll_ref[...] = -(quad + 0.5 * logs[0:1, 0:1]) / float(n_lead)
 
-    big = 2 * NB
+    big = tile
     for q in range(rows_total // big):
         o = q * big
         ch = chi_ref[o : o + big, :]
         acc = dot_f32(ch, p1_ref[...])
-        acc2 = dot_f32(ch, p2_ref[...]) + dot_f32(clo_ref[o : o + big, :], p3_ref[...])
+        acc2 = dot_f32(jnp.concatenate([ch, clo_ref[o : o + big, :]], axis=1), p23_ref[...])
         corr = acc[:, :NB] + (acc[:, NB:] + acc2[:, :NB])
         t, off = divmod(o, tile)
         gid = (t * row_procs + row_rank) * tile + off
@@ -332,7 +346,7 @@
         cid = n_lead + col_off + lax.broadcasted_iota(jnp.int32, (big, NB), 1)
         val = jnp.where(rid == cid, val + nugget, val) - corr
         slab_ref[o : o + big, :] = jnp.where(leading, 0.0, val)
-        for h in range(2):
+        for h in range(big // NB):
             at = off + h * NB
             tr = acc2[h * NB : (h + 1) * NB, NB:].T
             rest = obs_ref[t : t + 1, at : at + NB] - (tr[0:1, :] + tr[1:2, :])
@@ -349,20 +363,31 @@
     n_lead = 2 * tile
     width = n_lead + 2 * NB
     f32, bf16 = jnp.float32, jnp.bfloat16
-    mine = jnp.concatenate([coords[:, 0, :], observations[0:1, :]], axis=0)
-    lead = lax.all_gather(mine, "prow", axis=0)
+    procs = lax.axis_size("prow")
+    if procs <= 4 and procs & (procs - 1) == 0:
+        peers = procs - 1
+        gathered = [
+            lax.ppermute(x, "prow", [(r, r ^ m) for r in range(procs)])
+            for x in (coords, observations)
+            for m in range(1, procs)
+        ]
+    else:
+        peers = 0
+        mine = jnp.concatenate([coords[:, 0, :], observations[0:1, :]], axis=0)
+        gathered = [lax.all_gather(mine, "prow", axis=0)]
     vmem = pl.BlockSpec(memory_space=pltpu.VMEM)
     smem = pl.BlockSpec(memory_space=pltpu.SMEM)
     slab, white, ll = pl.pallas_call(
-        functools.partial(kernel, tile),
+        functools.partial(kernel, peers),
         out_shape=(
             jax.ShapeDtypeStruct((rows, SLAB_DEV), f32),
             jax.ShapeDtypeStruct((tile_count, tile), f32),
             jax.ShapeDtypeStruct((1, 1), f32),
         ),
-        in_specs=[smem, smem, vmem, vmem, vmem],
+        in_specs=[smem, smem] + [vmem] * (2 + len(gathered)),
         out_specs=(vmem, vmem, vmem),
         scratch_shapes=[
+            pltpu.VMEM((procs, 3, tile), f32),
             pltpu.VMEM((n_lead, width), f32),
             pltpu.VMEM((n_lead, NB), f32),
             pltpu.VMEM((n_lead, NB), f32),
@@ -370,17 +395,16 @@
             pltpu.VMEM((rows, n_lead), bf16),
             pltpu.VMEM((rows, n_lead), bf16),
             pltpu.VMEM((n_lead, 2 * NB), bf16),
-            pltpu.VMEM((n_lead, 2 * NB), bf16),
-            pltpu.VMEM((n_lead, 2 * NB), bf16),
+            pltpu.VMEM((2 * n_lead, 2 * NB), bf16),
             pltpu.VMEM((NB, NB), f32),
-            pltpu.VMEM((NB, 2 * NB), bf16),
-            pltpu.VMEM((NB, 2 * NB), bf16),
-            pltpu.VMEM((n_lead - NB, 2 * NB), bf16),
+            pltpu.VMEM((NB, 3 * NB), bf16),
+            pltpu.VMEM((NB, 3 * NB), bf16),
+            pltpu.VMEM((n_lead - NB, 3 * NB), bf16),
             pltpu.VMEM((NB, width), bf16),
             pltpu.VMEM((NB, width), bf16),
         ],
         compiler_params=pltpu.CompilerParams(vmem_limit_bytes=48 * 1024 * 1024),
-    )(length_scale, nugget, lead, coords.reshape(2, rows), observations)
+    )(length_scale, nugget, coords, observations, *gathered)
     return slab.reshape(tile_count, tile, SLAB_DEV), white, ll.reshape(1)
 
 

time: 59.5 us -> 59.5 us (level)
  blocking collectives: 6.2 us -> 0 us
  starting transfers between devices: 0 us -> 5.37 us
  waiting for transfers between devices: 0 us -> 1.89 us
  local copies, waits for them, and re-layouts: 2.98 us -> 1.47 us
  Pallas kernels: 47.9 us -> 48.5 us
    all_gather x1 -> x0, blocking collectives: 6.2 us -> none  [shards(): lead = lax.all_gather(mine, 'prow', axis=0)]
    ppermute x0 -> x6, starting transfers between devices: none -> 5.37 us  [shards(): lax.ppermute(x, 'prow', [(r, r ^ m) for r in range(procs)])]
    ppermute x0 -> x6, waiting for transfers between devices: none -> 1.89 us  [shards(): lax.ppermute(x, 'prow', [(r, r ^ m) for r in range(procs)])]
    slice x2 -> x0, local copies, waits for them, and re-layouts: 1.48 us -> none  [shards(): mine = jnp.concatenate([coords[:, 0, :], observations[0:1, :]], axis=0)]
  transfers between devices with their start and end apart: 0 -> 6, of which waited for: 0 -> 1; matrix products, arithmetic and copies ran while one was open for 0% -> 0% of each run, Pallas kernels for 0% -> 0%
where the time goes in v5:
time: 59.5 us; the launch traced here: 59.2 us
  Pallas kernels  48.5 us (82%)
  starting transfers between devices  5.37 us (9%)
  between operations  1.95 us (3%)
  waiting for transfers between devices  1.89 us (3%)
  local copies, waits for them, and re-layouts  1.47 us (2%)
    pallas_call x1, Pallas kernels, shards(): pl.pallas_call(functools.partial(kernel, peers), out_shape=(jax.ShapeDtyp...  48.5 us
    ppermute x6, starting transfers between devices, shards(): lax.ppermute(x, 'prow', [(r, r ^ m) for r in range(procs)])  5.37 us
    ppermute x6, waiting for transfers between devices, shards(): lax.ppermute(x, 'prow', [(r, r ^ m) for r in range(procs)])  1.89 us
    unnamed x4, local copies, waits for them, and re-layouts  1.47 us
  transfers between devices with their start and end apart: 6, of which 1 were waited for; matrix products, arithmetic and copies ran while one was open for 0% of the time, Pallas kernels for 0%

profile of v5, /device:TPU:0, one launch (start us, length us, event | category | flops | bytes accessed | tf_op | source)
XLA Modules:
  0.0 59.2 jit_solution(13914791582840361553)
XLA Ops:
  0.6 3.0 %collective-permute-start.4 = (f32[8,512]{1,0:T(8,128)}, f32[8,512]{1,0:T(8,128)S(1)}, u32[]{:S(2)}, u32[]{:S(2)}) collective-permute-start(f32[8,512]{1,0:T(8,128)} %obs_ref.1), channel_id=1, source_target_pairs={{0,16},{8,24},{16,0},{24,8},{1,17},{9,25},{17,1},{25,9},{2,18},{10... | collective-permute-start | bytes 49160 | tf_op jit(solution)/shard_map/ppermute | solution.py:370
  3.7 0.1 collective-permute-start.1
  3.7 0.0 collective-permute-start
  3.7 2.1 %collective-permute-start.2 = (f32[2,8,512]{2,1,0:T(8,128)}, f32[2,8,512]{2,1,0:T(8,128)S(1)}, u32[]{:S(2)}, u32[]{:S(2)}) collective-permute-start(f32[2,8,512]{2,1,0:T(8,128)} %loc_ref.1), channel_id=1, source_target_pairs={{0,24},{8,16},{16,8},{24,0},{1,25},{9,17},{17,9},{25,1},{2,26},{10... | collective-permute-start | bytes 98312 | tf_op jit(solution)/shard_map/ppermute | solution.py:370
  5.8 0.0 collective-permute-start.3
  5.8 0.0 collective-permute-done.4.refs_4_
  5.8 0.2 collective-permute-start.5
  7.3 0.0 collective-permute-done.3.refs_3_
  7.3 1.9 %collective-permute-done.5.refs_5_ = f32[8,512]{1,0:T(8,128)S(1)} collective-permute-done((f32[8,512]{1,0:T(8,128)}, f32[8,512]{1,0:T(8,128)S(1)}, u32[]{:S(2)}, u32[]{:S(2)}) %collective-permute-start.5) | collective-permute-done | bytes 16416 | tf_op jit(solution)/shard_map/ppermute | solution.py:370
  9.2 0.0 collective-permute-done.1.refs_1_
  9.2 0.0 collective-permute-done.refs_0_
  9.2 0.0 collective-permute-done.2.refs_2_
  9.2 0.0 copy-start
  9.2 0.7 %copy-done = f32[2,8,512]{2,1,0:T(8,128)S(1)} copy-done((f32[2,8,512]{2,1,0:T(8,128)S(1)}, f32[2,8,512]{2,1,0:T(8,128)}, u32[]{:S(2)}) %copy-start) | copy-done | bytes 32792
  10.0 0.0 copy-start.1
  10.0 0.7 %copy-done.1 = f32[8,512]{1,0:T(8,128)S(1)} copy-done((f32[8,512]{1,0:T(8,128)S(1)}, f32[8,512]{1,0:T(8,128)}, u32[]{:S(2)}) %copy-start.1) | copy-done | bytes 16408
  10.7 48.5 %shard_map.67 = (f32[4096,128]{1,0:T(8,128)}, f32[8,512]{1,0:T(8,128)}, f32[1,1]{1,0:T(1,128)}) custom-call(f32[1]{0:T(128)S(6)} %copy.7.ls_ref, f32[1]{0:T(128)S(6)} %copy.8.ng_ref, f32[2,8,512]{2,1,0:T(8,128)S(1)} %copy-done, f32[8,512]{1,0:T(8,128)S(1)} %copy-done.1, f32[2,8,512]{2,1,0:T(8,128)S(1)} %collective-permute-done.refs_0_, ...), custom_call_target="tpu_custom_call" | custom-call | tf_op jit(solution)/shard_map/pallas_call | solution.py:380
Async XLA Ops:
  0.6 5.2 %collective-permute-start.4 = (f32[8,512]{1,0:T(8,128)}, f32[8,512]{1,0:T(8,128)S(1)}, u32[]{:S(2)}, u32[]{:S(2)}) collective-permute-start(f32[8,512]{1,0:T(8,128)} %obs_ref.1), channel_id=1, source_target_pairs={{0,16},{8,24},{16,0},{24,8},{1,17},{9,25},{17,1},{25,9},{2,18},{10... | collective-permute-start | bytes 49160 | tf_op jit(solution)/shard_map/ppermute | solution.py:370
  3.7 5.5 %collective-permute-start.1 = (f32[2,8,512]{2,1,0:T(8,128)}, f32[2,8,512]{2,1,0:T(8,128)S(1)}, u32[]{:S(2)}, u32[]{:S(2)}) collective-permute-start(f32[2,8,512]{2,1,0:T(8,128)} %loc_ref.1), channel_id=1, source_target_pairs={{0,16},{8,24},{16,0},{24,8},{1,17},{9,25},{17,1},{25,9},{2,18},{10... | collective-permute-start | bytes 98312 | tf_op jit(solution)/shard_map/ppermute | solution.py:370
  3.7 5.5 %collective-permute-start = (f32[2,8,512]{2,1,0:T(8,128)}, f32[2,8,512]{2,1,0:T(8,128)S(1)}, u32[]{:S(2)}, u32[]{:S(2)}) collective-permute-start(f32[2,8,512]{2,1,0:T(8,128)} %loc_ref.1), channel_id=1, source_target_pairs={{0,8},{8,0},{16,24},{24,16},{1,9},{9,1},{17,25},{25,17},{2,10},{10... | collective-permute-start | bytes 98312 | tf_op jit(solution)/shard_map/ppermute | solution.py:370
  3.7 5.5 %collective-permute-start.2 = (f32[2,8,512]{2,1,0:T(8,128)}, f32[2,8,512]{2,1,0:T(8,128)S(1)}, u32[]{:S(2)}, u32[]{:S(2)}) collective-permute-start(f32[2,8,512]{2,1,0:T(8,128)} %loc_ref.1), channel_id=1, source_target_pairs={{0,24},{8,16},{16,8},{24,0},{1,25},{9,17},{17,9},{25,1},{2,26},{10... | collective-permute-start | bytes 98312 | tf_op jit(solution)/shard_map/ppermute | solution.py:370
  5.8 1.5 %collective-permute-start.3 = (f32[8,512]{1,0:T(8,128)}, f32[8,512]{1,0:T(8,128)S(1)}, u32[]{:S(2)}, u32[]{:S(2)}) collective-permute-start(f32[8,512]{1,0:T(8,128)} %obs_ref.1), channel_id=1, source_target_pairs={{0,8},{8,0},{16,24},{24,16},{1,9},{9,1},{17,25},{25,17},{2,10},{10... | collective-permute-start | bytes 49160 | tf_op jit(solution)/shard_map/ppermute | solution.py:370
  5.8 3.4 %collective-permute-start.5 = (f32[8,512]{1,0:T(8,128)}, f32[8,512]{1,0:T(8,128)S(1)}, u32[]{:S(2)}, u32[]{:S(2)}) collective-permute-start(f32[8,512]{1,0:T(8,128)} %obs_ref.1), channel_id=1, source_target_pairs={{0,24},{8,16},{16,8},{24,0},{1,25},{9,17},{17,9},{25,1},{2,26},{10... | collective-permute-start | bytes 49160 | tf_op jit(solution)/shard_map/ppermute | solution.py:370
  9.2 0.8 %copy-start = (f32[2,8,512]{2,1,0:T(8,128)S(1)}, f32[2,8,512]{2,1,0:T(8,128)}, u32[]{:S(2)}) copy-start(f32[2,8,512]{2,1,0:T(8,128)} %loc_ref.1) | copy-start | bytes 98308
  10.0 0.7 %copy-start.1 = (f32[8,512]{1,0:T(8,128)S(1)}, f32[8,512]{1,0:T(8,128)}, u32[]{:S(2)}) copy-start(f32[8,512]{1,0:T(8,128)} %obs_ref.1) | copy-start | bytes 49156

commit v6 on v5

--- a/solution.py
+++ b/solution.py
@@ -108,15 +108,15 @@
 
 
 def kernel(
-    peers, ls_ref, ng_ref, loc_ref, obs_ref, *refs,
+    peers, ls_ref, ng_ref, loc_ref, *refs,
 ):
-    gathered, refs = refs[: max(2 * peers, 1)], refs[max(2 * peers, 1) :]
+    gathered, refs = refs[: peers + 1], refs[peers + 1 :]
     (
         slab_ref, white_ref, ll_ref, lead_ref, a_ref, z_ref, site_ref, row_ref, chi_ref, clo_ref, p1_ref, p23_ref,
         d_ref, winv_ref, pinv_ref, col_ref, mh_ref, ml_ref,
     ) = refs
     f32, bf16 = jnp.float32, jnp.bfloat16
-    tile_count, tile = obs_ref.shape
+    tile_count, tile = loc_ref.shape[1:]
     n_lead = 2 * tile
     nblk = n_lead // NB
     width = n_lead + 2 * NB
@@ -126,13 +126,10 @@
     row_procs = lax.axis_size("prow")
     if peers:
         for t in range(peers + 1):
-            for c in range(3):
-                own = loc_ref[c, 0:1, :] if c < 2 else obs_ref[0:1, :]
-                for m in range(1, peers + 1):
-                    xy_ref, ob_ref = gathered[m - 1], gathered[peers + m - 1]
-                    theirs = xy_ref[c, 0:1, :] if c < 2 else ob_ref[0:1, :]
-                    own = jnp.where(row_rank == t ^ m, theirs, own)
-                lead_ref[t, c : c + 1, :] = own
+            rows = gathered[0][...]
+            for m in range(1, peers + 1):
+                rows = jnp.where(row_rank == t ^ m, gathered[m][...], rows)
+            lead_ref[t] = rows
     else:
         lead_ref[...] = gathered[0][...]
     ls = jnp.full((SUB, NB), ls_ref[0], f32)
@@ -182,7 +179,8 @@
         if key not in held:
             held[key] = []
             for h in range(2):
-                v = row_ref[pl.ds(pl.multiple_of(ro + h * SUB, SUB), SUB), :]
+                at = ro + h * SUB
+                v = row_ref[pl.ds(at if isinstance(at, int) else pl.multiple_of(at, SUB), SUB), :]
                 held[key].append((lane_bcast(v, 0), lane_bcast(v, 1)))
         t, u = divmod(j * NB, tile)
         vals = [
@@ -283,12 +281,14 @@
     out, logs = factor_block(load_rows(), planned(urgent, work))
     finish_block(out, True)
 
-    chunk = -(-rows_total // 16 // (nblk - 1)) * 16
+    big = 2 * NB
+    early_rows = rows_total * 3 // 4 // big * big
+    chunk = -(-early_rows // 16 // (nblk - 1)) * 16
     col_tiles = [(j * NB, min(j + 2, nblk) * NB) for j in range(1, nblk, 2)]
 
     def step(b, logs):
         held.clear()
-        base = jnp.minimum((b - 1) * chunk, rows_total - chunk)
+        base = jnp.minimum((b - 1) * chunk, early_rows - chunk)
         work = [
             functools.partial(
                 row_piece, pl.multiple_of(base + pair * 16, 16), ("row", pair), j
@@ -328,9 +328,17 @@
     quad = 0.5 * jnp.sum(jnp.where(first, z * z, 0.0), keepdims=True)
     ll_ref[...] = -(quad + 0.5 * logs[0:1, 0:1]) / float(n_lead)
 
-    big = tile
+    held.clear()
+    late = [
+        functools.partial(row_piece, ro, ("late", ro), j)
+        for ro in range(early_rows, rows_total, 16)
+        for j in range(nblk)
+    ]
+    turns = early_rows // big
     for q in range(rows_total // big):
         o = q * big
+        for f in late[len(late) * q // turns : len(late) * (q + 1) // turns]:
+            f()
         ch = chi_ref[o : o + big, :]
         acc = dot_f32(ch, p1_ref[...])
         acc2 = dot_f32(jnp.concatenate([ch, clo_ref[o : o + big, :]], axis=1), p23_ref[...])
@@ -349,7 +357,7 @@
         for h in range(big // NB):
             at = off + h * NB
             tr = acc2[h * NB : (h + 1) * NB, NB:].T
-            rest = obs_ref[t : t + 1, at : at + NB] - (tr[0:1, :] + tr[1:2, :])
+            rest = loc_ref[2, t : t + 1, at : at + NB] - (tr[0:1, :] + tr[1:2, :])
             if t == 0:
                 zs = pl.multiple_of(jnp.where(leading, gid, 0) + h * NB, NB)
                 zt = z_ref[pl.ds(zs, NB), :].T
@@ -364,16 +372,16 @@
     width = n_lead + 2 * NB
     f32, bf16 = jnp.float32, jnp.bfloat16
     procs = lax.axis_size("prow")
+    local = lax.optimization_barrier(jnp.concatenate([coords, observations[None]], axis=0))
+    mine = local[:, 0, :]
     if procs <= 4 and procs & (procs - 1) == 0:
         peers = procs - 1
-        gathered = [
-            lax.ppermute(x, "prow", [(r, r ^ m) for r in range(procs)])
-            for x in (coords, observations)
+        gathered = [mine] + [
+            lax.ppermute(mine, "prow", [(r, r ^ m) for r in range(procs)])
             for m in range(1, procs)
         ]
     else:
         peers = 0
-        mine = jnp.concatenate([coords[:, 0, :], observations[0:1, :]], axis=0)
         gathered = [lax.all_gather(mine, "prow", axis=0)]
     vmem = pl.BlockSpec(memory_space=pltpu.VMEM)
     smem = pl.BlockSpec(memory_space=pltpu.SMEM)
@@ -384,7 +392,7 @@
             jax.ShapeDtypeStruct((tile_count, tile), f32),
             jax.ShapeDtypeStruct((1, 1), f32),
         ),
-        in_specs=[smem, smem] + [vmem] * (2 + len(gathered)),
+        in_specs=[smem, smem, vmem] + [vmem] * len(gathered),
         out_specs=(vmem, vmem, vmem),
         scratch_shapes=[
             pltpu.VMEM((procs, 3, tile), f32),
@@ -404,7 +412,7 @@
             pltpu.VMEM((NB, width), bf16),
         ],
         compiler_params=pltpu.CompilerParams(vmem_limit_bytes=48 * 1024 * 1024),
-    )(length_scale, nugget, coords, observations, *gathered)
+    )(length_scale, nugget, local, *gathered)
     return slab.reshape(tile_count, tile, SLAB_DEV), white, ll.reshape(1)
 
 

time: 59.5 us -> 56.2 us (0.945)
  starting transfers between devices: 5.37 us -> 3.15 us
  Pallas kernels: 48.5 us -> 47.7 us
    ppermute x6 -> x3, starting transfers between devices: 5.37 us -> 3.15 us  [shards(): lax.ppermute(mine, 'prow', [(r, r ^ m) for r in range(procs)])]
    pallas_call x1, Pallas kernels: 48.5 us -> 47.7 us  [shards(): pl.pallas_call(functools.partial(kernel, peers), out_shape=(jax.ShapeDtyp...]
    broadcast_in_dim x0 -> x1, local copies, waits for them, and re-layouts: none -> 0.73 us  [shards(): observations[None]]
    unnamed x4 -> x1, local copies, waits for them, and re-layouts: 1.47 us -> 0.79 us
    ppermute x6 -> x3, waiting for transfers between devices: 1.89 us -> 1.65 us  [shards(): lax.ppermute(mine, 'prow', [(r, r ^ m) for r in range(procs)])]
  transfers between devices with their start and end apart: 6 -> 3, of which waited for: 1 -> 1; matrix products, arithmetic and copies ran while one was open for 0% -> 0% of each run, Pallas kernels for 0% -> 0%
where the time goes in v6:
time: 56.2 us; the launch traced here: 56 us
  Pallas kernels  47.7 us (85%)
  starting transfers between devices  3.15 us (6%)
  between operations  1.96 us (3%)
  waiting for transfers between devices  1.65 us (3%)
  local copies, waits for them, and re-layouts  1.54 us (3%)
    pallas_call x1, Pallas kernels, shards(): pl.pallas_call(functools.partial(kernel, peers), out_shape=(jax.ShapeDtyp...  47.7 us
    ppermute x3, starting transfers between devices, shards(): lax.ppermute(mine, 'prow', [(r, r ^ m) for r in range(procs)])  3.15 us
    ppermute x3, waiting for transfers between devices, shards(): lax.ppermute(mine, 'prow', [(r, r ^ m) for r in range(procs)])  1.65 us
  transfers between devices with their start and end apart: 3, of which 1 were waited for; matrix products, arithmetic and copies ran while one was open for 0% of the time, Pallas kernels for 0%

profile of v6, /device:TPU:0, one launch (start us, length us, event | category | flops | bytes accessed | tf_op | source)
XLA Modules:
  0.0 56.0 jit_solution(18321155855244654339)
XLA Ops:
  0.6 0.7 %broadcast_in_dim.3 = f32[1,8,512]{2,0,1:T(1,128)S(1)} reshape(f32[8,512]{1,0:T(8,128)} %param.5) | data formatting | bytes 32768 | tf_op jit(solution)/shard_map/broadcast_in_dim | solution.py:375
  1.4 0.8 %copy.7 = f32[2,8,512]{2,0,1:T(2,128)S(1)} copy(f32[2,8,512]{2,1,0:T(8,128)} %param.4) | data formatting | bytes 65536 | tf_op args[0]
  2.2 2.5 %collective-permute-start.2 = (f32[3,512]{1,0:T(4,128)S(1)}, f32[3,512]{1,0:T(4,128)S(1)}, u32[]{:S(2)}, u32[]{:S(2)}) collective-permute-start(f32[3,512]{1,0:T(4,128)S(1)} %slice_bitcast_fusion.refs_0_), channel_id=1, source_target_pairs={{0,24},{8,16},{16,8},{24,0},{1,25},{9,17},{17,9},{25,1},{2,26},{10... | collective-permute-start | bytes 18440 | tf_op jit(solution)/shard_map/ppermute | solution.py:380
  4.7 0.6 %collective-permute-start.1 = (f32[3,512]{1,0:T(4,128)S(1)}, f32[3,512]{1,0:T(4,128)S(1)}, u32[]{:S(2)}, u32[]{:S(2)}) collective-permute-start(f32[3,512]{1,0:T(4,128)S(1)} %slice_bitcast_fusion.refs_0_), channel_id=1, source_target_pairs={{0,16},{8,24},{16,0},{24,8},{1,17},{9,25},{17,1},{25,9},{2,18},{10... | collective-permute-start | bytes 18440 | tf_op jit(solution)/shard_map/ppermute | solution.py:380
  5.3 0.0 collective-permute-start
  6.7 0.0 collective-permute-done.2.refs_3_
  6.7 1.6 %collective-permute-done.1.refs_2_ = f32[3,512]{1,0:T(4,128)S(1)} collective-permute-done((f32[3,512]{1,0:T(4,128)S(1)}, f32[3,512]{1,0:T(4,128)S(1)}, u32[]{:S(2)}, u32[]{:S(2)}) %collective-permute-start.1) | collective-permute-done | bytes 6176 | tf_op jit(solution)/shard_map/ppermute | solution.py:380
  8.3 0.0 collective-permute-done.refs_1_
  8.3 47.7 %shard_map.67 = (f32[4096,128]{1,0:T(8,128)}, f32[8,512]{1,0:T(8,128)}, f32[1,1]{1,0:T(1,128)}) custom-call(f32[1]{0:T(128)S(6)} %copy.9.ls_ref, f32[1]{0:T(128)S(6)} %copy.10.ng_ref, f32[3,8,512]{2,1,0:T(8,128)S(1)} %copy.8.loc_ref, f32[3,512]{1,0:T(4,128)S(1)} %slice_bitcast_fusion.refs_0_, f32[3,512]{1,0:T(4,128)S(1)} %collective-permute-done.refs_1_, ...), custom_call_target="tpu_custom_call" | custom-call | tf_op jit(solution)/shard_map/pallas_call | solution.py:388
  (3 shorter events, 0.1 us)
Async XLA Ops:
  2.2 4.5 %collective-permute-start.2 = (f32[3,512]{1,0:T(4,128)S(1)}, f32[3,512]{1,0:T(4,128)S(1)}, u32[]{:S(2)}, u32[]{:S(2)}) collective-permute-start(f32[3,512]{1,0:T(4,128)S(1)} %slice_bitcast_fusion.refs_0_), channel_id=1, source_target_pairs={{0,24},{8,16},{16,8},{24,0},{1,25},{9,17},{17,9},{25,1},{2,26},{10... | collective-permute-start | bytes 18440 | tf_op jit(solution)/shard_map/ppermute | solution.py:380
  4.7 3.7 %collective-permute-start.1 = (f32[3,512]{1,0:T(4,128)S(1)}, f32[3,512]{1,0:T(4,128)S(1)}, u32[]{:S(2)}, u32[]{:S(2)}) collective-permute-start(f32[3,512]{1,0:T(4,128)S(1)} %slice_bitcast_fusion.refs_0_), channel_id=1, source_target_pairs={{0,16},{8,24},{16,0},{24,8},{1,17},{9,25},{17,1},{25,9},{2,18},{10... | collective-permute-start | bytes 18440 | tf_op jit(solution)/shard_map/ppermute | solution.py:380
  5.3 3.0 %collective-permute-start = (f32[3,512]{1,0:T(4,128)S(1)}, f32[3,512]{1,0:T(4,128)S(1)}, u32[]{:S(2)}, u32[]{:S(2)}) collective-permute-start(f32[3,512]{1,0:T(4,128)S(1)} %slice_bitcast_fusion.refs_0_), channel_id=1, source_target_pairs={{0,8},{8,0},{16,24},{24,16},{1,9},{9,1},{17,25},{25,17},{2,10},{10... | collective-permute-start | bytes 18440 | tf_op jit(solution)/shard_map/ppermute | solution.py:380

commit v7 on v6

--- a/solution.py
+++ b/solution.py
@@ -55,7 +55,7 @@
     out = []
     logs = jnp.zeros((SUB, NB), jnp.float32)
     cols = [lane_bcast(x_all[0], k) for k in range(SUB)]
-    d = row_bcast(cols[0], 0)
+    pivot = row_bcast(cols[0], 0), row_bcast(cols[1], 0), row_bcast(cols[1], 1)
     for s in range(groups):
         c0 = SUB * s
         more = s + 1 < groups
@@ -67,31 +67,53 @@
         x = jnp.where(here, (lane == sub + c0).astype(jnp.float32), x_all[s])
         x_out = jnp.zeros((SUB, NB), jnp.float32)
         prod = None
-        for k in range(SUB):
-            inv = pltpu.reciprocal(d, approx=True)
-            rs = lax.rsqrt(d)
-            prod = d if prod is None else prod * d
-            if k + 1 < SUB:
-                e = row_bcast(cols[k + 1], k)
-                d = row_bcast(cols[k + 1], k + 1) - (e * e) * inv
+        for k in range(0, SUB, 2):
+            a, b, c = pivot
+            det = a * c - b * b
+            inv = pltpu.reciprocal(det, approx=True)
+            prod = det if prod is None else prod * det
+            pairs = [(row_bcast(cols[m], k), row_bcast(cols[m], k + 1)) for m in range(k + 2, SUB)]
+            nxt = None
+            if k + 2 < SUB:
+                m0, m1 = cols[k + 2], cols[k + 3]
+                nxt = pairs[0], pairs[1], k + 2
             elif more:
-                e = row_bcast(low[k], 0)
-                d = row_bcast(ahead[0], 0) - (e * e) * inv
-            f = cols[k] - units[k]
-            fi = f * inv
-            h = low[k] * inv if more else None
-            for m in range(k + 1, SUB):
-                e = row_bcast(cols[m], k)
-                cols[m] = cols[m] - ((f * e) * inv if m <= k + 2 else fi * e)
+                m0, m1 = ahead[0], ahead[1]
+                nxt = [(row_bcast(low[k], m), row_bcast(low[k + 1], m)) for m in range(2)] + [0]
+            if nxt is not None:
+                (p0, q0), (p1, q1), at = nxt
+                u0, v0 = c * p0 - b * q0, a * q0 - b * p0
+                u1, v1 = c * p1 - b * q1, a * q1 - b * p1
+                pivot = (
+                    row_bcast(m0, at) - (u0 * p0 + v0 * q0) * inv,
+                    row_bcast(m1, at) - (u0 * p1 + v0 * q1) * inv,
+                    row_bcast(m1, at + 1) - (u1 * p1 + v1 * q1) * inv,
+                )
+            f0, f1 = cols[k] - units[k], cols[k + 1] - units[k + 1]
+            g0, g1 = f0 * c - f1 * b, f1 * a - f0 * b
+            e0, e1 = g0 * inv, g1 * inv
+            if more:
+                l0, l1 = low[k], low[k + 1]
+                h0, h1 = (l0 * c - l1 * b) * inv, (l1 * a - l0 * b) * inv
+            for m in range(k + 2, SUB):
+                p, q = pairs[m - k - 2]
+                cols[m] = cols[m] - (
+                    (g0 * p + g1 * q) * inv if m < k + 4 else e0 * p + e1 * q
+                )
                 if more:
-                    low[m] = low[m] - h * e
+                    low[m] = low[m] - (h0 * p + h1 * q)
             if more:
                 for m in range(SUB):
-                    ahead[m] = ahead[m] - h * row_bcast(low[k], m)
-            xk = row_bcast(x, k)
-            x_out = jnp.where(sub == k, xk * rs, x_out)
-            x = x - fi * xk
+                    ahead[m] = ahead[m] - (h0 * row_bcast(l0, m) + h1 * row_bcast(l1, m))
+            x0, x1 = row_bcast(x, k), row_bcast(x, k + 1)
+            rs0 = lax.rsqrt(a)
+            inv_a = rs0 * rs0
+            rs1 = lax.rsqrt(det * inv_a)
+            x_out = jnp.where(sub == k, x0 * rs0, x_out)
+            x_out = jnp.where(sub == k + 1, (x1 - (b * inv_a) * x0) * rs1, x_out)
+            x = x - (e0 * x0 + e1 * x1)
             fill(s, k)
+            fill(s, k + 1)
         logs = logs + jnp.log(prod)
         out.append(jnp.where(lane < c0 + SUB, x_out, 0.0) if more else x_out)
         if more:

time: 56.2 us -> 57.5 us (1.023)
  Pallas kernels: 47.7 us -> 48.9 us
    pallas_call x1, Pallas kernels: 47.7 us -> 48.9 us  [shards(): pl.pallas_call(functools.partial(kernel, peers), out_shape=(jax.ShapeDtyp...]
where the time goes in v7:
time: 57.5 us; the launch traced here: 57.3 us
  Pallas kernels  48.9 us (85%)
  starting transfers between devices  3.15 us (5%)
  between operations  1.96 us (3%)
  waiting for transfers between devices  1.65 us (3%)
  local copies, waits for them, and re-layouts  1.54 us (3%)
    pallas_call x1, Pallas kernels, shards(): pl.pallas_call(functools.partial(kernel, peers), out_shape=(jax.ShapeDtyp...  48.9 us
    ppermute x3, starting transfers between devices, shards(): lax.ppermute(mine, 'prow', [(r, r ^ m) for r in range(procs)])  3.15 us
    ppermute x3, waiting for transfers between devices, shards(): lax.ppermute(mine, 'prow', [(r, r ^ m) for r in range(procs)])  1.65 us
  transfers between devices with their start and end apart: 3, of which 1 were waited for; matrix products, arithmetic and copies ran while one was open for 0% of the time, Pallas kernels for 0%

profile of v7, /device:TPU:0, one launch (start us, length us, event | category | flops | bytes accessed | tf_op | source)
XLA Modules:
  0.0 57.3 jit_solution(8818687991895253125)
XLA Ops:
  0.6 0.7 %broadcast_in_dim.3 = f32[1,8,512]{2,0,1:T(1,128)S(1)} reshape(f32[8,512]{1,0:T(8,128)} %param.5) | data formatting | bytes 32768 | tf_op jit(solution)/shard_map/broadcast_in_dim | solution.py:397
  1.4 0.8 %copy.7 = f32[2,8,512]{2,0,1:T(2,128)S(1)} copy(f32[2,8,512]{2,1,0:T(8,128)} %param.4) | data formatting | bytes 65536 | tf_op args[0]
  2.2 2.5 %collective-permute-start.2 = (f32[3,512]{1,0:T(4,128)S(1)}, f32[3,512]{1,0:T(4,128)S(1)}, u32[]{:S(2)}, u32[]{:S(2)}) collective-permute-start(f32[3,512]{1,0:T(4,128)S(1)} %slice_bitcast_fusion.refs_0_), channel_id=1, source_target_pairs={{0,24},{8,16},{16,8},{24,0},{1,25},{9,17},{17,9},{25,1},{2,26},{10... | collective-permute-start | bytes 18440 | tf_op jit(solution)/shard_map/ppermute | solution.py:402
  4.7 0.6 %collective-permute-start.1 = (f32[3,512]{1,0:T(4,128)S(1)}, f32[3,512]{1,0:T(4,128)S(1)}, u32[]{:S(2)}, u32[]{:S(2)}) collective-permute-start(f32[3,512]{1,0:T(4,128)S(1)} %slice_bitcast_fusion.refs_0_), channel_id=1, source_target_pairs={{0,16},{8,24},{16,0},{24,8},{1,17},{9,25},{17,1},{25,9},{2,18},{10... | collective-permute-start | bytes 18440 | tf_op jit(solution)/shard_map/ppermute | solution.py:402
  5.3 0.0 collective-permute-start
  6.7 0.0 collective-permute-done.2.refs_3_
  6.7 1.6 %collective-permute-done.1.refs_2_ = f32[3,512]{1,0:T(4,128)S(1)} collective-permute-done((f32[3,512]{1,0:T(4,128)S(1)}, f32[3,512]{1,0:T(4,128)S(1)}, u32[]{:S(2)}, u32[]{:S(2)}) %collective-permute-start.1) | collective-permute-done | bytes 6176 | tf_op jit(solution)/shard_map/ppermute | solution.py:402
  8.3 0.0 collective-permute-done.refs_1_
  8.3 48.9 %shard_map.67 = (f32[4096,128]{1,0:T(8,128)}, f32[8,512]{1,0:T(8,128)}, f32[1,1]{1,0:T(1,128)}) custom-call(f32[1]{0:T(128)S(6)} %copy.9.ls_ref, f32[1]{0:T(128)S(6)} %copy.10.ng_ref, f32[3,8,512]{2,1,0:T(8,128)S(1)} %copy.8.loc_ref, f32[3,512]{1,0:T(4,128)S(1)} %slice_bitcast_fusion.refs_0_, f32[3,512]{1,0:T(4,128)S(1)} %collective-permute-done.refs_1_, ...), custom_call_target="tpu_custom_call" | custom-call | tf_op jit(solution)/shard_map/pallas_call | solution.py:410
  (3 shorter events, 0.1 us)
Async XLA Ops:
  2.2 4.5 %collective-permute-start.2 = (f32[3,512]{1,0:T(4,128)S(1)}, f32[3,512]{1,0:T(4,128)S(1)}, u32[]{:S(2)}, u32[]{:S(2)}) collective-permute-start(f32[3,512]{1,0:T(4,128)S(1)} %slice_bitcast_fusion.refs_0_), channel_id=1, source_target_pairs={{0,24},{8,16},{16,8},{24,0},{1,25},{9,17},{17,9},{25,1},{2,26},{10... | collective-permute-start | bytes 18440 | tf_op jit(solution)/shard_map/ppermute | solution.py:402
  4.7 3.7 %collective-permute-start.1 = (f32[3,512]{1,0:T(4,128)S(1)}, f32[3,512]{1,0:T(4,128)S(1)}, u32[]{:S(2)}, u32[]{:S(2)}) collective-permute-start(f32[3,512]{1,0:T(4,128)S(1)} %slice_bitcast_fusion.refs_0_), channel_id=1, source_target_pairs={{0,16},{8,24},{16,0},{24,8},{1,17},{9,25},{17,1},{25,9},{2,18},{10... | collective-permute-start | bytes 18440 | tf_op jit(solution)/shard_map/ppermute | solution.py:402
  5.3 3.0 %collective-permute-start = (f32[3,512]{1,0:T(4,128)S(1)}, f32[3,512]{1,0:T(4,128)S(1)}, u32[]{:S(2)}, u32[]{:S(2)}) collective-permute-start(f32[3,512]{1,0:T(4,128)S(1)} %slice_bitcast_fusion.refs_0_), channel_id=1, source_target_pairs={{0,8},{8,0},{16,24},{24,16},{1,9},{9,1},{17,25},{25,17},{2,10},{10... | collective-permute-start | bytes 18440 | tf_op jit(solution)/shard_map/ppermute | solution.py:402

commit v8 on v6

--- a/solution.py
+++ b/solution.py
@@ -1,4 +1,5 @@
 import functools
+import math
 
 import jax
 import jax.numpy as jnp
@@ -10,6 +11,7 @@
 SLAB_DEV = 128
 NB = 128
 SUB = 8
+AHEAD = 4
 
 
 def lane_bcast(v, c):
@@ -33,11 +35,11 @@
 LOG2E = 1.4426950408889634
 
 
-def matern(dx, dy, rate2):
-    t = (dx * dx + dy * dy) * rate2
-    s = t * lax.rsqrt(jnp.maximum(t, 1e-30))
-    e = jnp.exp2(s * -LOG2E)
-    return e + s * e
+def matern(dx, dy, rate):
+    d2 = dx * dx + dy * dy
+    dist = d2 * lax.rsqrt(jnp.maximum(d2, 1e-30))
+    e = jnp.exp2(dist * rate[1])
+    return e + (dist * rate[0]) * e
 
 
 def tree_sum(xs):
@@ -60,11 +62,12 @@
         c0 = SUB * s
         more = s + 1 < groups
         if more:
-            g_next = [lane_bcast(x_all[s + 1], c0 + k) for k in range(SUB)]
-            low = list(g_next)
-            ahead = [lane_bcast(x_all[s + 1], c0 + SUB + k) for k in range(SUB)]
+            low = [lane_bcast(x_all[s + 1], c0 + k) for k in range(SUB)]
+            ahead = [lane_bcast(x_all[s + 1], c0 + SUB + k) for k in range(AHEAD)]
         here = (lane >= c0) & (lane < c0 + SUB)
         x = jnp.where(here, (lane == sub + c0).astype(jnp.float32), x_all[s])
+        if more:
+            x_next = jnp.where(here, 0.0, x_all[s + 1])
         x_out = jnp.zeros((SUB, NB), jnp.float32)
         prod = None
         for k in range(SUB):
@@ -86,9 +89,11 @@
                 if more:
                     low[m] = low[m] - h * e
             if more:
-                for m in range(SUB):
+                for m in range(AHEAD):
                     ahead[m] = ahead[m] - h * row_bcast(low[k], m)
             xk = row_bcast(x, k)
+            if more:
+                x_next = x_next - h * xk
             x_out = jnp.where(sub == k, xk * rs, x_out)
             x = x - fi * xk
             fill(s, k)
@@ -96,14 +101,13 @@
         out.append(jnp.where(lane < c0 + SUB, x_out, 0.0) if more else x_out)
         if more:
             x_rows = [row_bcast(x, k) for k in range(SUB)]
-            for t in range(s + 1, groups):
-                g = g_next if t == s + 1 else [
-                    lane_bcast(x_all[t], c0 + k) for k in range(SUB)
-                ]
+            for t in range(s + 2, groups):
+                g = [lane_bcast(x_all[t], c0 + k) for k in range(SUB)]
                 x_all[t] = jnp.where(here, 0.0, x_all[t]) - tree_sum(
                     [g[k] * x_rows[k] for k in range(SUB)]
                 )
-            cols = ahead
+            x_all[s + 1] = x_next
+            cols = ahead + [lane_bcast(x_next, c0 + SUB + k) for k in range(AHEAD, SUB)]
     return out, logs
 
 
@@ -112,7 +116,7 @@
 ):
     gathered, refs = refs[: peers + 1], refs[peers + 1 :]
     (
-        slab_ref, white_ref, ll_ref, lead_ref, a_ref, z_ref, site_ref, row_ref, chi_ref, clo_ref, p1_ref, p23_ref,
+        slab_hbm, white_ref, ll_ref, slab_ref, sems, lead_ref, a_ref, z_ref, site_ref, row_ref, chi_ref, clo_ref, p1_ref, p23_ref,
         d_ref, winv_ref, pinv_ref, col_ref, mh_ref, ml_ref,
     ) = refs
     f32, bf16 = jnp.float32, jnp.bfloat16
@@ -133,7 +137,8 @@
     else:
         lead_ref[...] = gathered[0][...]
     ls = jnp.full((SUB, NB), ls_ref[0], f32)
-    rate2 = 3.0 / (ls * ls)
+    decay = math.sqrt(3.0) / ls
+    rate = decay, decay * -LOG2E
     nugget = ng_ref[0]
     col_off = col_rank * SLAB_DEV
     col_tile = 2 + col_off // tile
@@ -166,11 +171,11 @@
         x, y, ob = held["site", o]
         if j < nblk:
             t, u = divmod(j * NB, tile)
-            val = matern(x - lead_ref[t, 0:1, u : u + NB], y - lead_ref[t, 1:2, u : u + NB], rate2)
+            val = matern(x - lead_ref[t, 0:1, u : u + NB], y - lead_ref[t, 1:2, u : u + NB], rate)
             if j == b:
                 val = jnp.where(lane == sub + g * SUB, val + nugget, val)
         elif j == nblk:
-            val = matern(x - cx, y - cy, rate2)
+            val = matern(x - cx, y - cy, rate)
         else:
             val = jnp.where(lane < 2, ob, 0.0)
         a_ref[o : o + SUB, j * NB : (j + 1) * NB] = val
@@ -184,7 +189,7 @@
                 held[key].append((lane_bcast(v, 0), lane_bcast(v, 1)))
         t, u = divmod(j * NB, tile)
         vals = [
-            matern(x - lead_ref[t, 0:1, u : u + NB], y - lead_ref[t, 1:2, u : u + NB], rate2)
+            matern(x - lead_ref[t, 0:1, u : u + NB], y - lead_ref[t, 1:2, u : u + NB], rate)
             for x, y in held[key]
         ]
         hi, lo = split2(jnp.concatenate(vals, axis=0))
@@ -284,9 +289,9 @@
     big = 2 * NB
     early_rows = rows_total * 3 // 4 // big * big
     chunk = -(-early_rows // 16 // (nblk - 1)) * 16
-    col_tiles = [(j * NB, min(j + 2, nblk) * NB) for j in range(1, nblk, 2)]
-
-    def step(b, logs):
+
+    def step(upto, b, logs):
+        col_tiles = [(j * NB, min(j + 2, upto) * NB) for j in range(1, upto, 2)]
         held.clear()
         base = jnp.minimum((b - 1) * chunk, early_rows - chunk)
         work = [
@@ -305,7 +310,9 @@
         finish_block(out, True)
         return logs + more
 
-    logs = lax.fori_loop(1, nblk, step, logs)
+    mid = nblk // 2
+    logs = lax.fori_loop(1, mid, functools.partial(step, nblk), logs)
+    logs = lax.fori_loop(mid, nblk, functools.partial(step, nblk - mid + 1), logs)
     column_parts()
     keep_z(n_lead - NB)
     for f in tile_pieces(n_lead, width, 0):
@@ -335,6 +342,7 @@
         for j in range(nblk)
     ]
     turns = early_rows // big
+    copies = []
     for q in range(rows_total // big):
         o = q * big
         for f in late[len(late) * q // turns : len(late) * (q + 1) // turns]:
@@ -349,11 +357,17 @@
         v = row_ref[o : o + big, :]
         x = jnp.broadcast_to(v[:, 0:1], (big, NB))
         y = jnp.broadcast_to(v[:, 1:2], (big, NB))
-        val = matern(x - cx, y - cy, rate2[0:1, :])
+        val = matern(x - cx, y - cy, (rate[0][0:1, :], rate[1][0:1, :]))
         rid = gid + lax.broadcasted_iota(jnp.int32, (big, NB), 0)
         cid = n_lead + col_off + lax.broadcasted_iota(jnp.int32, (big, NB), 1)
         val = jnp.where(rid == cid, val + nugget, val) - corr
         slab_ref[o : o + big, :] = jnp.where(leading, 0.0, val)
+        copies.append(
+            pltpu.make_async_copy(
+                slab_ref.at[pl.ds(o, big)], slab_hbm.at[pl.ds(o, big)], sems.at[q]
+            )
+        )
+        copies[-1].start()
         for h in range(big // NB):
             at = off + h * NB
             tr = acc2[h * NB : (h + 1) * NB, NB:].T
@@ -363,6 +377,8 @@
                 zt = z_ref[pl.ds(zs, NB), :].T
                 rest = jnp.where(leading, zt[0:1, :], rest)
             white_ref[t : t + 1, at : at + NB] = rest
+    for copy in copies:
+        copy.wait()
 
 
 def shards(coords, observations, length_scale, nugget):
@@ -393,8 +409,10 @@
             jax.ShapeDtypeStruct((1, 1), f32),
         ),
         in_specs=[smem, smem, vmem] + [vmem] * len(gathered),
-        out_specs=(vmem, vmem, vmem),
+        out_specs=(pl.BlockSpec(memory_space=pl.ANY), vmem, vmem),
         scratch_shapes=[
+            pltpu.VMEM((rows, SLAB_DEV), f32),
+            pltpu.SemaphoreType.DMA((rows // (2 * NB),)),
             pltpu.VMEM((procs, 3, tile), f32),
             pltpu.VMEM((n_lead, width), f32),
             pltpu.VMEM((n_lead, NB), f32),

time: 56.2 us -> 60.8 us (1.082)
  Pallas kernels: 47.7 us -> 52 us
    pallas_call x1, Pallas kernels: 47.7 us -> 52 us  [shards(): pl.pallas_call(functools.partial(kernel, peers), out_shape=(jax.ShapeDtyp...]
where the time goes in v8:
time: 60.8 us; the launch traced here: 60.5 us
  Pallas kernels  52 us (86%)
  starting transfers between devices  3.15 us (5%)
  between operations  2.14 us (4%)
  waiting for transfers between devices  1.65 us (3%)
  local copies, waits for them, and re-layouts  1.54 us (3%)
    pallas_call x1, Pallas kernels, shards(): pl.pallas_call(functools.partial(kernel, peers), out_shape=(jax.ShapeDtyp...  52 us
    ppermute x3, starting transfers between devices, shards(): lax.ppermute(mine, 'prow', [(r, r ^ m) for r in range(procs)])  3.15 us
    ppermute x3, waiting for transfers between devices, shards(): lax.ppermute(mine, 'prow', [(r, r ^ m) for r in range(procs)])  1.65 us
  transfers between devices with their start and end apart: 3, of which 1 were waited for; matrix products, arithmetic and copies ran while one was open for 0% of the time, Pallas kernels for 0%

profile of v8, /device:TPU:0, one launch (start us, length us, event | category | flops | bytes accessed | tf_op | source)
XLA Modules:
  0.0 60.5 jit_solution(9263781805720208928)
XLA Ops:
  0.6 0.7 %broadcast_in_dim.3 = f32[1,8,512]{2,0,1:T(1,128)S(1)} reshape(f32[8,512]{1,0:T(8,128)} %param.5) | data formatting | bytes 32768 | tf_op jit(solution)/shard_map/broadcast_in_dim | solution.py:391
  1.4 0.8 %copy.7 = f32[2,8,512]{2,0,1:T(2,128)S(1)} copy(f32[2,8,512]{2,1,0:T(8,128)} %param.4) | data formatting | bytes 65536 | tf_op args[0]
  2.2 2.5 %collective-permute-start.2 = (f32[3,512]{1,0:T(4,128)S(1)}, f32[3,512]{1,0:T(4,128)S(1)}, u32[]{:S(2)}, u32[]{:S(2)}) collective-permute-start(f32[3,512]{1,0:T(4,128)S(1)} %slice_bitcast_fusion.refs_0_), channel_id=1, source_target_pairs={{0,24},{8,16},{16,8},{24,0},{1,25},{9,17},{17,9},{25,1},{2,26},{10... | collective-permute-start | bytes 18440 | tf_op jit(solution)/shard_map/ppermute | solution.py:396
  4.7 0.6 %collective-permute-start.1 = (f32[3,512]{1,0:T(4,128)S(1)}, f32[3,512]{1,0:T(4,128)S(1)}, u32[]{:S(2)}, u32[]{:S(2)}) collective-permute-start(f32[3,512]{1,0:T(4,128)S(1)} %slice_bitcast_fusion.refs_0_), channel_id=1, source_target_pairs={{0,16},{8,24},{16,0},{24,8},{1,17},{9,25},{17,1},{25,9},{2,18},{10... | collective-permute-start | bytes 18440 | tf_op jit(solution)/shard_map/ppermute | solution.py:396
  5.3 0.0 collective-permute-start
  6.7 0.0 collective-permute-done.2.refs_3_
  6.7 1.6 %collective-permute-done.1.refs_2_ = f32[3,512]{1,0:T(4,128)S(1)} collective-permute-done((f32[3,512]{1,0:T(4,128)S(1)}, f32[3,512]{1,0:T(4,128)S(1)}, u32[]{:S(2)}, u32[]{:S(2)}) %collective-permute-start.1) | collective-permute-done | bytes 6176 | tf_op jit(solution)/shard_map/ppermute | solution.py:396
  8.3 0.0 collective-permute-done.refs_1_
  8.3 52.0 %shard_map.67 = (f32[4096,128]{1,0:T(8,128)}, f32[8,512]{1,0:T(8,128)}, f32[1,1]{1,0:T(1,128)}) custom-call(f32[1]{0:T(128)S(6)} %copy.9.ls_ref, f32[1]{0:T(128)S(6)} %copy.10.ng_ref, f32[3,8,512]{2,1,0:T(8,128)S(1)} %copy.8.loc_ref, f32[3,512]{1,0:T(4,128)S(1)} %slice_bitcast_fusion.refs_0_, f32[3,512]{1,0:T(4,128)S(1)} %collective-permute-done.refs_1_, ...), custom_call_target="tpu_custom_call" | custom-call | tf_op jit(solution)/shard_map/pallas_call | solution.py:404
  (3 shorter events, 0.1 us)
Async XLA Ops:
  2.2 4.5 %collective-permute-start.2 = (f32[3,512]{1,0:T(4,128)S(1)}, f32[3,512]{1,0:T(4,128)S(1)}, u32[]{:S(2)}, u32[]{:S(2)}) collective-permute-start(f32[3,512]{1,0:T(4,128)S(1)} %slice_bitcast_fusion.refs_0_), channel_id=1, source_target_pairs={{0,24},{8,16},{16,8},{24,0},{1,25},{9,17},{17,9},{25,1},{2,26},{10... | collective-permute-start | bytes 18440 | tf_op jit(solution)/shard_map/ppermute | solution.py:396
  4.7 3.7 %collective-permute-start.1 = (f32[3,512]{1,0:T(4,128)S(1)}, f32[3,512]{1,0:T(4,128)S(1)}, u32[]{:S(2)}, u32[]{:S(2)}) collective-permute-start(f32[3,512]{1,0:T(4,128)S(1)} %slice_bitcast_fusion.refs_0_), channel_id=1, source_target_pairs={{0,16},{8,24},{16,0},{24,8},{1,17},{9,25},{17,1},{25,9},{2,18},{10... | collective-permute-start | bytes 18440 | tf_op jit(solution)/shard_map/ppermute | solution.py:396
  5.3 3.0 %collective-permute-start = (f32[3,512]{1,0:T(4,128)S(1)}, f32[3,512]{1,0:T(4,128)S(1)}, u32[]{:S(2)}, u32[]{:S(2)}) collective-permute-start(f32[3,512]{1,0:T(4,128)S(1)} %slice_bitcast_fusion.refs_0_), channel_id=1, source_target_pairs={{0,8},{8,0},{16,24},{24,16},{1,9},{9,1},{17,25},{25,17},{2,10},{10... | collective-permute-start | bytes 18440 | tf_op jit(solution)/shard_map/ppermute | solution.py:396

commit v9 on v6

--- a/solution.py
+++ b/solution.py
@@ -1,4 +1,5 @@
 import functools
+import math
 
 import jax
 import jax.numpy as jnp
@@ -33,11 +34,11 @@
 LOG2E = 1.4426950408889634
 
 
-def matern(dx, dy, rate2):
-    t = (dx * dx + dy * dy) * rate2
-    s = t * lax.rsqrt(jnp.maximum(t, 1e-30))
-    e = jnp.exp2(s * -LOG2E)
-    return e + s * e
+def matern(dx, dy, rate):
+    d2 = dx * dx + dy * dy
+    dist = d2 * lax.rsqrt(jnp.maximum(d2, 1e-30))
+    e = jnp.exp2(dist * rate[1])
+    return e + (dist * rate[0]) * e
 
 
 def tree_sum(xs):
@@ -112,7 +113,7 @@
 ):
     gathered, refs = refs[: peers + 1], refs[peers + 1 :]
     (
-        slab_ref, white_ref, ll_ref, lead_ref, a_ref, z_ref, site_ref, row_ref, chi_ref, clo_ref, p1_ref, p23_ref,
+        slab_hbm, white_ref, ll_ref, slab_ref, sems, lead_ref, a_ref, z_ref, site_ref, row_ref, chi_ref, clo_ref, p1_ref, p23_ref,
         d_ref, winv_ref, pinv_ref, col_ref, mh_ref, ml_ref,
     ) = refs
     f32, bf16 = jnp.float32, jnp.bfloat16
@@ -133,7 +134,8 @@
     else:
         lead_ref[...] = gathered[0][...]
     ls = jnp.full((SUB, NB), ls_ref[0], f32)
-    rate2 = 3.0 / (ls * ls)
+    decay = math.sqrt(3.0) / ls
+    rate = decay, decay * -LOG2E
     nugget = ng_ref[0]
     col_off = col_rank * SLAB_DEV
     col_tile = 2 + col_off // tile
@@ -166,11 +168,11 @@
         x, y, ob = held["site", o]
         if j < nblk:
             t, u = divmod(j * NB, tile)
-            val = matern(x - lead_ref[t, 0:1, u : u + NB], y - lead_ref[t, 1:2, u : u + NB], rate2)
+            val = matern(x - lead_ref[t, 0:1, u : u + NB], y - lead_ref[t, 1:2, u : u + NB], rate)
             if j == b:
                 val = jnp.where(lane == sub + g * SUB, val + nugget, val)
         elif j == nblk:
-            val = matern(x - cx, y - cy, rate2)
+            val = matern(x - cx, y - cy, rate)
         else:
             val = jnp.where(lane < 2, ob, 0.0)
         a_ref[o : o + SUB, j * NB : (j + 1) * NB] = val
@@ -184,7 +186,7 @@
                 held[key].append((lane_bcast(v, 0), lane_bcast(v, 1)))
         t, u = divmod(j * NB, tile)
         vals = [
-            matern(x - lead_ref[t, 0:1, u : u + NB], y - lead_ref[t, 1:2, u : u + NB], rate2)
+            matern(x - lead_ref[t, 0:1, u : u + NB], y - lead_ref[t, 1:2, u : u + NB], rate)
             for x, y in held[key]
         ]
         hi, lo = split2(jnp.concatenate(vals, axis=0))
@@ -281,14 +283,12 @@
     out, logs = factor_block(load_rows(), planned(urgent, work))
     finish_block(out, True)
 
-    big = 2 * NB
-    early_rows = rows_total * 3 // 4 // big * big
-    chunk = -(-early_rows // 16 // (nblk - 1)) * 16
+    chunk = -(-rows_total // 16 // (nblk - 1)) * 16
     col_tiles = [(j * NB, min(j + 2, nblk) * NB) for j in range(1, nblk, 2)]
 
     def step(b, logs):
         held.clear()
-        base = jnp.minimum((b - 1) * chunk, early_rows - chunk)
+        base = jnp.minimum((b - 1) * chunk, rows_total - chunk)
         work = [
             functools.partial(
                 row_piece, pl.multiple_of(base + pair * 16, 16), ("row", pair), j
@@ -328,41 +328,45 @@
     quad = 0.5 * jnp.sum(jnp.where(first, z * z, 0.0), keepdims=True)
     ll_ref[...] = -(quad + 0.5 * logs[0:1, 0:1]) / float(n_lead)
 
-    held.clear()
-    late = [
-        functools.partial(row_piece, ro, ("late", ro), j)
-        for ro in range(early_rows, rows_total, 16)
-        for j in range(nblk)
-    ]
-    turns = early_rows // big
-    for q in range(rows_total // big):
-        o = q * big
-        for f in late[len(late) * q // turns : len(late) * (q + 1) // turns]:
-            f()
-        ch = chi_ref[o : o + big, :]
+    def slab_copy(t):
+        o = pl.multiple_of(t * tile, tile)
+        return pltpu.make_async_copy(
+            slab_ref.at[pl.ds(o, tile)], slab_hbm.at[pl.ds(o, tile)], sems.at[t]
+        )
+
+    tile_row = lax.broadcasted_iota(jnp.int32, (tile_count, NB), 0)
+
+    def finish(t, carry):
+        o = pl.multiple_of(t * tile, tile)
+        ch = chi_ref[pl.ds(o, tile), :]
         acc = dot_f32(ch, p1_ref[...])
-        acc2 = dot_f32(jnp.concatenate([ch, clo_ref[o : o + big, :]], axis=1), p23_ref[...])
+        acc2 = dot_f32(jnp.concatenate([ch, clo_ref[pl.ds(o, tile), :]], axis=1), p23_ref[...])
         corr = acc[:, :NB] + (acc[:, NB:] + acc2[:, :NB])
-        t, off = divmod(o, tile)
-        gid = (t * row_procs + row_rank) * tile + off
+        gid = (t * row_procs + row_rank) * tile
         leading = gid < n_lead
-        v = row_ref[o : o + big, :]
-        x = jnp.broadcast_to(v[:, 0:1], (big, NB))
-        y = jnp.broadcast_to(v[:, 1:2], (big, NB))
-        val = matern(x - cx, y - cy, rate2[0:1, :])
-        rid = gid + lax.broadcasted_iota(jnp.int32, (big, NB), 0)
-        cid = n_lead + col_off + lax.broadcasted_iota(jnp.int32, (big, NB), 1)
+        v = row_ref[pl.ds(o, tile), :]
+        x = jnp.broadcast_to(v[:, 0:1], (tile, NB))
+        y = jnp.broadcast_to(v[:, 1:2], (tile, NB))
+        val = matern(x - cx, y - cy, (rate[0][0:1, :], rate[1][0:1, :]))
+        rid = gid + lax.broadcasted_iota(jnp.int32, (tile, NB), 0)
+        cid = n_lead + col_off + lax.broadcasted_iota(jnp.int32, (tile, NB), 1)
         val = jnp.where(rid == cid, val + nugget, val) - corr
-        slab_ref[o : o + big, :] = jnp.where(leading, 0.0, val)
-        for h in range(big // NB):
-            at = off + h * NB
-            tr = acc2[h * NB : (h + 1) * NB, NB:].T
-            rest = loc_ref[2, t : t + 1, at : at + NB] - (tr[0:1, :] + tr[1:2, :])
-            if t == 0:
-                zs = pl.multiple_of(jnp.where(leading, gid, 0) + h * NB, NB)
-                zt = z_ref[pl.ds(zs, NB), :].T
-                rest = jnp.where(leading, zt[0:1, :], rest)
-            white_ref[t : t + 1, at : at + NB] = rest
+        slab_ref[pl.ds(o, tile), :] = jnp.where(leading, 0.0, val)
+        slab_copy(t).start()
+        for h in range(tile // NB):
+            at = h * NB
+            tr = acc2[at : at + NB, NB:].T
+            rest = loc_ref[2, :, at : at + NB] - (tr[0:1, :] + tr[1:2, :])
+            zs = pl.multiple_of(jnp.where(leading, gid, 0) + at, NB)
+            zt = z_ref[pl.ds(zs, NB), :].T
+            rest = jnp.where(leading, zt[0:1, :], rest)
+            kept = white_ref[:, at : at + NB]
+            white_ref[:, at : at + NB] = jnp.where(tile_row == t, rest, kept)
+        return carry
+
+    lax.fori_loop(0, tile_count, finish, 0)
+    for t in range(tile_count):
+        slab_copy(t).wait()
 
 
 def shards(coords, observations, length_scale, nugget):
@@ -393,8 +397,10 @@
             jax.ShapeDtypeStruct((1, 1), f32),
         ),
         in_specs=[smem, smem, vmem] + [vmem] * len(gathered),
-        out_specs=(vmem, vmem, vmem),
+        out_specs=(pl.BlockSpec(memory_space=pl.ANY), vmem, vmem),
         scratch_shapes=[
+            pltpu.VMEM((rows, SLAB_DEV), f32),
+            pltpu.SemaphoreType.DMA((tile_count,)),
             pltpu.VMEM((procs, 3, tile), f32),
             pltpu.VMEM((n_lead, width), f32),
             pltpu.VMEM((n_lead, NB), f32),

time: 56.2 us -> 58.3 us (1.037)
  Pallas kernels: 47.7 us -> 49.7 us
    pallas_call x1, Pallas kernels: 47.7 us -> 49.7 us  [shards(): pl.pallas_call(functools.partial(kernel, peers), out_shape=(jax.ShapeDtyp...]
where the time goes in v9:
time: 58.3 us; the launch traced here: 58 us
  Pallas kernels  49.7 us (85%)
  starting transfers between devices  3.15 us (5%)
  between operations  1.96 us (3%)
  waiting for transfers between devices  1.65 us (3%)
  local copies, waits for them, and re-layouts  1.54 us (3%)
    pallas_call x1, Pallas kernels, shards(): pl.pallas_call(functools.partial(kernel, peers), out_shape=(jax.ShapeDtyp...  49.7 us
    ppermute x3, starting transfers between devices, shards(): lax.ppermute(mine, 'prow', [(r, r ^ m) for r in range(procs)])  3.15 us
    ppermute x3, waiting for transfers between devices, shards(): lax.ppermute(mine, 'prow', [(r, r ^ m) for r in range(procs)])  1.65 us
  transfers between devices with their start and end apart: 3, of which 1 were waited for; matrix products, arithmetic and copies ran while one was open for 0% of the time, Pallas kernels for 0%

profile of v9, /device:TPU:0, one launch (start us, length us, event | category | flops | bytes accessed | tf_op | source)
XLA Modules:
  0.0 58.0 jit_solution(3470556923189075123)
XLA Ops:
  0.6 0.7 %broadcast_in_dim.3 = f32[1,8,512]{2,0,1:T(1,128)S(1)} reshape(f32[8,512]{1,0:T(8,128)} %param.5) | data formatting | bytes 32768 | tf_op jit(solution)/shard_map/broadcast_in_dim | solution.py:379
  1.4 0.8 %copy.7 = f32[2,8,512]{2,0,1:T(2,128)S(1)} copy(f32[2,8,512]{2,1,0:T(8,128)} %param.4) | data formatting | bytes 65536 | tf_op args[0]
  2.2 2.5 %collective-permute-start.2 = (f32[3,512]{1,0:T(4,128)S(1)}, f32[3,512]{1,0:T(4,128)S(1)}, u32[]{:S(2)}, u32[]{:S(2)}) collective-permute-start(f32[3,512]{1,0:T(4,128)S(1)} %slice_bitcast_fusion.refs_0_), channel_id=1, source_target_pairs={{0,24},{8,16},{16,8},{24,0},{1,25},{9,17},{17,9},{25,1},{2,26},{10... | collective-permute-start | bytes 18440 | tf_op jit(solution)/shard_map/ppermute | solution.py:384
  4.7 0.6 %collective-permute-start.1 = (f32[3,512]{1,0:T(4,128)S(1)}, f32[3,512]{1,0:T(4,128)S(1)}, u32[]{:S(2)}, u32[]{:S(2)}) collective-permute-start(f32[3,512]{1,0:T(4,128)S(1)} %slice_bitcast_fusion.refs_0_), channel_id=1, source_target_pairs={{0,16},{8,24},{16,0},{24,8},{1,17},{9,25},{17,1},{25,9},{2,18},{10... | collective-permute-start | bytes 18440 | tf_op jit(solution)/shard_map/ppermute | solution.py:384
  5.3 0.0 collective-permute-start
  6.7 0.0 collective-permute-done.2.refs_3_
  6.7 1.6 %collective-permute-done.1.refs_2_ = f32[3,512]{1,0:T(4,128)S(1)} collective-permute-done((f32[3,512]{1,0:T(4,128)S(1)}, f32[3,512]{1,0:T(4,128)S(1)}, u32[]{:S(2)}, u32[]{:S(2)}) %collective-permute-start.1) | collective-permute-done | bytes 6176 | tf_op jit(solution)/shard_map/ppermute | solution.py:384
  8.3 0.0 collective-permute-done.refs_1_
  8.3 49.7 %shard_map.67 = (f32[4096,128]{1,0:T(8,128)}, f32[8,512]{1,0:T(8,128)}, f32[1,1]{1,0:T(1,128)}) custom-call(f32[1]{0:T(128)S(6)} %copy.9.ls_ref, f32[1]{0:T(128)S(6)} %copy.10.ng_ref, f32[3,8,512]{2,1,0:T(8,128)S(1)} %copy.8.loc_ref, f32[3,512]{1,0:T(4,128)S(1)} %slice_bitcast_fusion.refs_0_, f32[3,512]{1,0:T(4,128)S(1)} %collective-permute-done.refs_1_, ...), custom_call_target="tpu_custom_call" | custom-call | tf_op jit(solution)/shard_map/pallas_call | solution.py:392
  (3 shorter events, 0.1 us)
Async XLA Ops:
  2.2 4.5 %collective-permute-start.2 = (f32[3,512]{1,0:T(4,128)S(1)}, f32[3,512]{1,0:T(4,128)S(1)}, u32[]{:S(2)}, u32[]{:S(2)}) collective-permute-start(f32[3,512]{1,0:T(4,128)S(1)} %slice_bitcast_fusion.refs_0_), channel_id=1, source_target_pairs={{0,24},{8,16},{16,8},{24,0},{1,25},{9,17},{17,9},{25,1},{2,26},{10... | collective-permute-start | bytes 18440 | tf_op jit(solution)/shard_map/ppermute | solution.py:384
  4.7 3.7 %collective-permute-start.1 = (f32[3,512]{1,0:T(4,128)S(1)}, f32[3,512]{1,0:T(4,128)S(1)}, u32[]{:S(2)}, u32[]{:S(2)}) collective-permute-start(f32[3,512]{1,0:T(4,128)S(1)} %slice_bitcast_fusion.refs_0_), channel_id=1, source_target_pairs={{0,16},{8,24},{16,0},{24,8},{1,17},{9,25},{17,1},{25,9},{2,18},{10... | collective-permute-start | bytes 18440 | tf_op jit(solution)/shard_map/ppermute | solution.py:384
  5.3 3.0 %collective-permute-start = (f32[3,512]{1,0:T(4,128)S(1)}, f32[3,512]{1,0:T(4,128)S(1)}, u32[]{:S(2)}, u32[]{:S(2)}) collective-permute-start(f32[3,512]{1,0:T(4,128)S(1)} %slice_bitcast_fusion.refs_0_), channel_id=1, source_target_pairs={{0,8},{8,0},{16,24},{24,16},{1,9},{9,1},{17,25},{25,17},{2,10},{10... | collective-permute-start | bytes 18440 | tf_op jit(solution)/shard_map/ppermute | solution.py:384

commit v10 on v6

--- a/solution.py
+++ b/solution.py
@@ -60,10 +60,14 @@
         c0 = SUB * s
         more = s + 1 < groups
         if more:
-            g_next = [lane_bcast(x_all[s + 1], c0 + k) for k in range(SUB)]
-            low = list(g_next)
+            low = [lane_bcast(x_all[s + 1], c0 + k) for k in range(SUB)]
             ahead = [lane_bcast(x_all[s + 1], c0 + SUB + k) for k in range(SUB)]
         here = (lane >= c0) & (lane < c0 + SUB)
+        near = range(s + 1, min(s + 3, groups))
+        lows = [list(low)] if more else []
+        if s + 2 < groups:
+            lows.append([lane_bcast(x_all[s + 2], c0 + k) for k in range(SUB)])
+        x_near = [jnp.where(here, 0.0, x_all[t]) for t in near]
         x = jnp.where(here, (lane == sub + c0).astype(jnp.float32), x_all[s])
         x_out = jnp.zeros((SUB, NB), jnp.float32)
         prod = None
@@ -75,20 +79,21 @@
                 e = row_bcast(cols[k + 1], k)
                 d = row_bcast(cols[k + 1], k + 1) - (e * e) * inv
             elif more:
-                e = row_bcast(low[k], 0)
+                e = row_bcast(lows[0][k], 0)
                 d = row_bcast(ahead[0], 0) - (e * e) * inv
             f = cols[k] - units[k]
             fi = f * inv
-            h = low[k] * inv if more else None
+            hs = [low[k] * inv for low in lows]
             for m in range(k + 1, SUB):
                 e = row_bcast(cols[m], k)
                 cols[m] = cols[m] - ((f * e) * inv if m <= k + 2 else fi * e)
-                if more:
+                for low, h in zip(lows, hs):
                     low[m] = low[m] - h * e
             if more:
                 for m in range(SUB):
-                    ahead[m] = ahead[m] - h * row_bcast(low[k], m)
+                    ahead[m] = ahead[m] - hs[0] * row_bcast(lows[0][k], m)
             xk = row_bcast(x, k)
+            x_near = [v - h * xk for v, h in zip(x_near, hs)]
             x_out = jnp.where(sub == k, xk * rs, x_out)
             x = x - fi * xk
             fill(s, k)
@@ -96,10 +101,10 @@
         out.append(jnp.where(lane < c0 + SUB, x_out, 0.0) if more else x_out)
         if more:
             x_rows = [row_bcast(x, k) for k in range(SUB)]
-            for t in range(s + 1, groups):
-                g = g_next if t == s + 1 else [
-                    lane_bcast(x_all[t], c0 + k) for k in range(SUB)
-                ]
+            for t, v in zip(near, x_near):
+                x_all[t] = v
+            for t in range(s + 3, groups):
+                g = [lane_bcast(x_all[t], c0 + k) for k in range(SUB)]
                 x_all[t] = jnp.where(here, 0.0, x_all[t]) - tree_sum(
                     [g[k] * x_rows[k] for k in range(SUB)]
                 )

time: 56.2 us -> 56.2 us (level)
  no operation moved by 1% of the time
where the time goes in v10:
time: 56.2 us; the launch traced here: 56 us
  Pallas kernels  47.6 us (85%)
  starting transfers between devices  3.15 us (6%)
  between operations  1.96 us (3%)
  waiting for transfers between devices  1.65 us (3%)
  local copies, waits for them, and re-layouts  1.54 us (3%)
    pallas_call x1, Pallas kernels, shards(): pl.pallas_call(functools.partial(kernel, peers), out_shape=(jax.ShapeDtyp...  47.6 us
    ppermute x3, starting transfers between devices, shards(): lax.ppermute(mine, 'prow', [(r, r ^ m) for r in range(procs)])  3.15 us
    ppermute x3, waiting for transfers between devices, shards(): lax.ppermute(mine, 'prow', [(r, r ^ m) for r in range(procs)])  1.65 us
  transfers between devices with their start and end apart: 3, of which 1 were waited for; matrix products, arithmetic and copies ran while one was open for 0% of the time, Pallas kernels for 0%

profile of v10, /device:TPU:0, one launch (start us, length us, event | category | flops | bytes accessed | tf_op | source)
XLA Modules:
  0.0 56.0 jit_solution(4661043181952121480)
XLA Ops:
  0.6 0.7 %broadcast_in_dim.3 = f32[1,8,512]{2,0,1:T(1,128)S(1)} reshape(f32[8,512]{1,0:T(8,128)} %param.5) | data formatting | bytes 32768 | tf_op jit(solution)/shard_map/broadcast_in_dim | solution.py:380
  1.4 0.8 %copy.7 = f32[2,8,512]{2,0,1:T(2,128)S(1)} copy(f32[2,8,512]{2,1,0:T(8,128)} %param.4) | data formatting | bytes 65536 | tf_op args[0]
  2.2 2.5 %collective-permute-start.2 = (f32[3,512]{1,0:T(4,128)S(1)}, f32[3,512]{1,0:T(4,128)S(1)}, u32[]{:S(2)}, u32[]{:S(2)}) collective-permute-start(f32[3,512]{1,0:T(4,128)S(1)} %slice_bitcast_fusion.refs_0_), channel_id=1, source_target_pairs={{0,24},{8,16},{16,8},{24,0},{1,25},{9,17},{17,9},{25,1},{2,26},{10... | collective-permute-start | bytes 18440 | tf_op jit(solution)/shard_map/ppermute | solution.py:385
  4.7 0.6 %collective-permute-start.1 = (f32[3,512]{1,0:T(4,128)S(1)}, f32[3,512]{1,0:T(4,128)S(1)}, u32[]{:S(2)}, u32[]{:S(2)}) collective-permute-start(f32[3,512]{1,0:T(4,128)S(1)} %slice_bitcast_fusion.refs_0_), channel_id=1, source_target_pairs={{0,16},{8,24},{16,0},{24,8},{1,17},{9,25},{17,1},{25,9},{2,18},{10... | collective-permute-start | bytes 18440 | tf_op jit(solution)/shard_map/ppermute | solution.py:385
  5.3 0.0 collective-permute-start
  6.7 0.0 collective-permute-done.2.refs_3_
  6.7 1.6 %collective-permute-done.1.refs_2_ = f32[3,512]{1,0:T(4,128)S(1)} collective-permute-done((f32[3,512]{1,0:T(4,128)S(1)}, f32[3,512]{1,0:T(4,128)S(1)}, u32[]{:S(2)}, u32[]{:S(2)}) %collective-permute-start.1) | collective-permute-done | bytes 6176 | tf_op jit(solution)/shard_map/ppermute | solution.py:385
  8.3 0.0 collective-permute-done.refs_1_
  8.3 47.6 %shard_map.67 = (f32[4096,128]{1,0:T(8,128)}, f32[8,512]{1,0:T(8,128)}, f32[1,1]{1,0:T(1,128)}) custom-call(f32[1]{0:T(128)S(6)} %copy.9.ls_ref, f32[1]{0:T(128)S(6)} %copy.10.ng_ref, f32[3,8,512]{2,1,0:T(8,128)S(1)} %copy.8.loc_ref, f32[3,512]{1,0:T(4,128)S(1)} %slice_bitcast_fusion.refs_0_, f32[3,512]{1,0:T(4,128)S(1)} %collective-permute-done.refs_1_, ...), custom_call_target="tpu_custom_call" | custom-call | tf_op jit(solution)/shard_map/pallas_call | solution.py:393
  (3 shorter events, 0.1 us)
Async XLA Ops:
  2.2 4.5 %collective-permute-start.2 = (f32[3,512]{1,0:T(4,128)S(1)}, f32[3,512]{1,0:T(4,128)S(1)}, u32[]{:S(2)}, u32[]{:S(2)}) collective-permute-start(f32[3,512]{1,0:T(4,128)S(1)} %slice_bitcast_fusion.refs_0_), channel_id=1, source_target_pairs={{0,24},{8,16},{16,8},{24,0},{1,25},{9,17},{17,9},{25,1},{2,26},{10... | collective-permute-start | bytes 18440 | tf_op jit(solution)/shard_map/ppermute | solution.py:385
  4.7 3.7 %collective-permute-start.1 = (f32[3,512]{1,0:T(4,128)S(1)}, f32[3,512]{1,0:T(4,128)S(1)}, u32[]{:S(2)}, u32[]{:S(2)}) collective-permute-start(f32[3,512]{1,0:T(4,128)S(1)} %slice_bitcast_fusion.refs_0_), channel_id=1, source_target_pairs={{0,16},{8,24},{16,0},{24,8},{1,17},{9,25},{17,1},{25,9},{2,18},{10... | collective-permute-start | bytes 18440 | tf_op jit(solution)/shard_map/ppermute | solution.py:385
  5.3 3.0 %collective-permute-start = (f32[3,512]{1,0:T(4,128)S(1)}, f32[3,512]{1,0:T(4,128)S(1)}, u32[]{:S(2)}, u32[]{:S(2)}) collective-permute-start(f32[3,512]{1,0:T(4,128)S(1)} %slice_bitcast_fusion.refs_0_), channel_id=1, source_target_pairs={{0,8},{8,0},{16,24},{24,16},{1,9},{9,1},{17,25},{25,17},{2,10},{10... | collective-permute-start | bytes 18440 | tf_op jit(solution)/shard_map/ppermute | solution.py:385
